TPU v7x, 256 devices: a whole 4x4x8 slice. The times are simulated.
256 devices in a mesh: dp: 4 (over x), expert: 8 (over z), etp: 8 (over y, core).
Axes of the slice: x: 4, y: 4, z: 8, core: 2. Of those that a mesh axis runs over, the one named last changes fastest.
Arguments:
- grad_output: bfloat16 [2048, 6144], P(('dp', 'expert', 'etp')), may hold values from -6 to 6
- comb_weights: bfloat16 [2048, 4], P(('dp', 'expert', 'etp')), may hold values from 0.099609375 to 1
- expert_ids: int32 [2048, 4], P(('dp', 'expert', 'etp')), may hold values from 0 to 7, all different within a row; in each aligned block of 8 rows (0 to 7, 8 to 15, ...) at most 6 rows name the same one
- down_weight: bfloat16 [8, 6144, 6144], P('expert', 'etp', 'dp'), may hold values from -0.078125 to 0.078125
- gate_weight: bfloat16 [8, 6144, 6144], P('expert', 'dp', 'etp'), may hold values from -0.078125 to 0.078125
- up_weight: bfloat16 [8, 6144, 6144], P('expert', 'dp', 'etp'), may hold values from -0.078125 to 0.078125
- gate_saved: bfloat16 [8, 1536, 6144], P('expert', None, 'etp'), may hold values from -6 to 6
- up_saved: bfloat16 [8, 1536, 6144], P('expert', None, 'etp'), may hold values from -6 to 6
Outputs:
- input_grad: bfloat16 [2048, 6144], P(('dp', 'expert', 'etp'))
Inputs may be any that keep to these rules, and one draw needn't show every extreme that they name: `expert_ids`: each token names 4 different experts; no expert is named by more than 6 of the tokens of one device.
All inputs are finite; a program needn't handle non-finite values.
Results may differ from a plain program's by a relative error of at most 0.0049.
Values may be sent and summed in bfloat16 or wider, within the bound.
A program may use at most 128 MiB of HBM per device.

v0:
```python
import jax
import jax.numpy as jnp
from jax import lax
from jax.sharding import PartitionSpec as P


def swiglu_backward(hidden_raw, weight, gate_pre, up_pre):
    gate_value = gate_pre.astype(jnp.float32)
    up_value = up_pre.astype(jnp.float32)
    sigmoid_gate = jax.nn.sigmoid(gate_value)
    scaled = hidden_raw * weight[:, None]
    gate_grad = (
        scaled * up_value * sigmoid_gate * (1.0 + gate_value * (1.0 - sigmoid_gate))
    ).astype(jnp.bfloat16)
    up_grad = (scaled * gate_value * sigmoid_gate).astype(jnp.bfloat16)
    return (gate_grad, up_grad)


def on_device(
    grad_output, comb_weights, expert_ids, down_weight, gate_weight, up_weight, gate_saved, up_saved
):
    group_count = lax.axis_size("dp")
    expert_count = lax.axis_size("expert")
    tensor_count = lax.axis_size("etp")
    tokens_here, model_width = grad_output.shape
    choices_count = expert_ids.shape[1]
    capacity = min(
        tokens_here, tokens_here * choices_count // expert_count + max(2, tokens_here // 6)
    )
    quarter = model_width // group_count
    labels = jnp.arange(expert_count, dtype=jnp.int32)
    matches = (expert_ids[:, :, None] == labels[None, None, :]).astype(jnp.int32)
    expert_hits = jnp.sum(matches, axis=1)
    before = jnp.cumsum(expert_hits, axis=0) - expert_hits
    position = jnp.sum(matches * before[:, None, :], axis=2)
    target = expert_ids * capacity + position
    slot_labels = jnp.arange(expert_count * capacity, dtype=jnp.int32)
    chosen = slot_labels[:, None, None] == target[None, :, :]
    selector = (
        jnp.any(chosen, axis=2).astype(jnp.bfloat16).reshape(expert_count, capacity, tokens_here)
    )
    pieces = grad_output.reshape(tokens_here, group_count, quarter)
    outgoing = jnp.einsum(
        "ect,tqd->eqcd", selector, pieces, preferred_element_type=jnp.float32
    ).astype(jnp.bfloat16)
    weight_slots = jnp.sum(
        jnp.where(chosen, comb_weights.astype(jnp.float32)[None, :, :], 0.0), axis=(1, 2)
    )
    weight_out = jnp.broadcast_to(
        weight_slots.reshape(expert_count, 1, capacity), (expert_count, group_count, capacity)
    ).astype(jnp.bfloat16)
    arrived, arrived_weight = (
        lax.all_to_all(outgoing, "dp", split_axis=1, concat_axis=1, tiled=True),
        lax.all_to_all(weight_out, "dp", split_axis=1, concat_axis=1, tiled=True),
    )
    copied = jnp.broadcast_to(
        arrived[:, None], (expert_count, tensor_count, group_count, capacity, quarter)
    )
    copied = copied.reshape(expert_count * tensor_count, group_count, capacity, quarter)
    copied_weight = jnp.broadcast_to(
        arrived_weight[:, None], (expert_count, tensor_count, group_count, capacity)
    )
    copied_weight = copied_weight.reshape(expert_count * tensor_count, group_count, capacity)
    routed, routed_weight = (
        lax.all_to_all(copied, ("expert", "etp"), split_axis=0, concat_axis=0, tiled=True),
        lax.all_to_all(copied_weight, ("expert", "etp"), split_axis=0, concat_axis=0, tiled=True),
    )
    slot_total = expert_count * tensor_count * group_count * capacity
    routed = routed.reshape(slot_total, quarter)
    slot_weight = routed_weight.reshape(slot_total).astype(jnp.float32)
    down_local = down_weight[0]
    gate_local = gate_saved[0]
    up_local = up_saved[0]
    partial_value = jnp.einsum("sq,fq->sf", routed, down_local, preferred_element_type=jnp.float32)
    hidden_raw = lax.psum(partial_value, "dp")
    gate_grad, up_grad = swiglu_backward(hidden_raw, slot_weight, gate_local, up_local)
    slot_grad = jnp.einsum(
        "sf,qf->sq", gate_grad, gate_weight[0], preferred_element_type=jnp.float32
    )
    slot_grad = slot_grad + jnp.einsum(
        "sf,qf->sq", up_grad, up_weight[0], preferred_element_type=jnp.float32
    )
    outbound = slot_grad.reshape(expert_count * tensor_count, group_count, capacity, quarter)
    inbound = lax.all_to_all(outbound, ("expert", "etp"), split_axis=0, concat_axis=0, tiled=True)
    inbound = jnp.sum(
        inbound.reshape(expert_count, tensor_count, group_count, capacity, quarter), axis=1
    )
    complete = lax.all_to_all(inbound, "dp", split_axis=1, concat_axis=3, tiled=True)
    complete = complete.reshape(expert_count * capacity, model_width)
    picked = jnp.take(complete, target.reshape(-1), axis=0)
    picked = picked.reshape(tokens_here, choices_count, model_width)
    return jnp.sum(picked, axis=1).astype(jnp.bfloat16)


def solution(mesh):
    in_specs = (
        P(("dp", "expert", "etp"), None),
        P(("dp", "expert", "etp"), None),
        P(("dp", "expert", "etp"), None),
        P("expert", "etp", "dp"),
        P("expert", "dp", "etp"),
        P("expert", "dp", "etp"),
        P("expert", None, "etp"),
        P("expert", None, "etp"),
    )
    out_specs = P(("dp", "expert", "etp"), None)
    return jax.shard_map(
        on_device, mesh=mesh, in_specs=in_specs, out_specs=out_specs, check_vma=False
    )
```

profile of v0, /device:TPU:1, one launch (start us, length us, event | category | flops | bytes accessed | tf_op | source)
XLA Modules:
  0.0 573.3 jit_solution(5975261550007912184)
XLA Ops:
  6.5 0.9 convert_reduce_fusion
  7.5 0.9 select_reduce_fusion.2
  9.4 1.2 fusion.9
  10.6 13.6 %all_to_all.40 = bf16[8,4,6,1536]{3,0,2,1:T(8,128)(2,1)S(1)} all-to-all(bf16[8,4,6,1536]{3,0,2,1:T(8,128)(2,1)S(1)} %copy.52), channel_id=1, replica_groups=mesh['dp'=4,'expert'=8,'etp'=8] {'dp'}, dimensions={1} | all-to-all | bytes 1179648 | tf_op jit(solution)/shard_map/all_to_all | solution.py:53
  24.7 1.4 broadcast_in_dim.26
  26.1 121.3 %all_to_all.41 = bf16[64,4,6,1536]{3,1,2,0:T(4,128)(2,1)S(1)} all-to-all(bf16[64,4,6,1536]{3,1,2,0:T(4,128)(2,1)S(1)} %bitcast.46), channel_id=1, replica_groups=mesh['dp'=4,'expert'=8,'etp'=8] {'expert','etp'}, dimensions={0} | all-to-all | bytes 9437184 | tf_op jit(solution)/shard_map/all_to_all | solution.py:65
  147.4 4.4 copy.54
  151.8 8.5 %reshape.100 = bf16[1536,1536]{1,0:T(8,128)(2,1)} reshape(bf16[64,4,6,1536]{3,2,1,0:T(8,128)(2,1)} %copy.54) | data formatting | bytes 9437184 | tf_op jit(solution)/shard_map/reshape | solution.py:69
  160.3 9.2 %fusion.16 = f32[1536,768]{1,0:T(8,128)} fusion(bf16[1536,1536]{1,0:T(8,128)(2,1)} %reshape.100, bf16[1,768,1536]{2,1,0:T(8,128)(2,1)} %param.11), kind=kOutput, calls=%fused_computation.22 | convolution fusion | flops 3623878656 | bytes 11796480 | tf_op jit(solution)/shard_map/sq,fq->sf/dot_general | solution.py:74
  170.3 6.5 %all_to_all.42 = bf16[8,4,6]{2,0,1:T(8,128)(2,1)S(1)} all-to-all(bf16[8,4,6]{2,0,1:T(8,128)(2,1)S(1)} %broadcast_in_dim.50), channel_id=1, replica_groups=mesh['dp'=4,'expert'=8,'etp'=8] {'dp'}, dimensions={1} | all-to-all | bytes 768 | tf_op jit(solution)/shard_map/all_to_all | solution.py:54
  176.9 16.7 %all_to_all.43 = bf16[64,4,6]{2,1,0:T(4,128)(2,1)S(1)} all-to-all(bf16[64,4,6]{2,1,0:T(4,128)(2,1)S(1)} %bitcast.49), channel_id=1, replica_groups=mesh['dp'=4,'expert'=8,'etp'=8] {'expert','etp'}, dimensions={0} | all-to-all | bytes 6144 | tf_op jit(solution)/shard_map/all_to_all | solution.py:66
  193.7 76.8 %all-reduce.2.cloned.1.call-done = f32[1536,768]{1,0:T(8,128)} async-done(((f32[1536,768]{1,0:T(8,128)}), f32[1536,768]{1,0:T(8,128)}) %all-reduce.2.cloned.1.call-update) | async-done | bytes 4718608 | tf_op jit(solution)/shard_map/psum | solution.py:75
  270.5 12.6 %fusion.12 = f32[1536,1536]{1,0:T(8,128)} fusion(bf16[1,1536,768]{2,1,0:T(8,128)(2,1)S(1)} %copy-done, f32[1536,768]{1,0:T(8,128)} %all-reduce.2.cloned.1.call-done, bf16[1,1536,768]{2,1,0:T(8,128)(2,1)} %param.15, bf16[1,1536,768]{2,1,0:T(8,128)(2,1)} %param.14, f32[1536]{0:T(1024)S(1)} %reshape.106), kind=kOutput, calls=%fused_computation.19 | convolution fusion | flops 3639214080 | bytes 21239808 | tf_op jit(solution)/shard_map/sf,qf->sq/dot_general | solution.py:77
  283.1 9.5 %convolution_add_fusion = f32[1536,1536]{1,0:T(8,128)} fusion(f32[1536,1536]{1,0:T(8,128)} %fusion.12, f32[1536,768]{1,0:T(8,128)S(1)} %copy-done.3, bf16[1,1536,768]{2,1,0:T(8,128)(2,1)S(1)} %copy-done.5, bf16[1,1536,768]{2,1,0:T(8,128)(2,1)S(1)} %copy-done.4, f32[1536]{0:T(1024)S(1)} %reshape.106), kind=kOutput, calls=%fused_computation.2 | convolution fusion | flops 3635675136 | bytes 28317696 | tf_op jit(solution)/shard_map/sf,qf->sq/dot_general | solution.py:80
  292.6 11.4 %reshape.102 = f32[64,4,6,1536]{3,2,1,0:T(8,128)} reshape(f32[1536,1536]{1,0:T(8,128)} %convolution_add_fusion) | data formatting | bytes 18874368 | tf_op jit(solution)/shard_map/reshape | solution.py:83
  304.0 17.0 %copy.56 = f32[64,4,6,1536]{3,1,2,0:T(4,128)} copy(f32[64,4,6,1536]{3,2,1,0:T(8,128)} %reshape.102) | data formatting | bytes 18874368 | tf_op jit(solution)/shard_map/reshape | solution.py:83
  320.9 218.3 %all_to_all.44 = f32[64,4,6,1536]{3,1,2,0:T(4,128)S(1)} all-to-all(f32[64,4,6,1536]{3,1,2,0:T(4,128)} %copy.56), channel_id=1, replica_groups=mesh['dp'=4,'expert'=8,'etp'=8] {'expert','etp'}, dimensions={0} | all-to-all | bytes 18874368 | tf_op jit(solution)/shard_map/all_to_all | solution.py:84
  539.3 1.5 bitcast_reduce_fusion
  540.8 1.7 copy.58
  542.5 3.5 all-to-all-start.5
  546.3 14.8 %all-to-all-done.5 = f32[8,4,6,1536]{3,0,2,1:T(8,128)S(1)} async-done(((f32[8,4,6,1536]{3,0,2,1:T(8,128)}), f32[8,4,6,1536]{3,0,2,1:T(8,128)S(1)}, u32[]{:S(2)}, u32[]{:S(2)}) %all-to-all-start.5) | async-done | bytes 1179680 | tf_op jit(solution)/shard_map/all_to_all | solution.py:88
  562.2 1.7 gather_fusion
  563.8 1.4 gather.7
  565.2 1.2 select_reduce_fusion
  (36 shorter events, 4.0 us)
Async XLA Ops:
  6.5 264.0 %copy-start = (bf16[1,1536,768]{2,1,0:T(8,128)(2,1)S(1)}, bf16[1,1536,768]{2,1,0:T(8,128)(2,1)}, u32[]{:S(2)}) copy-start(bf16[1,1536,768]{2,1,0:T(8,128)(2,1)} %param.12) | copy-start | bytes 7077892
  6.5 264.0 %all-reduce.2.cloned.1.call-start = ((), (), s32[]{:S(2)}) async-start(), calls=%async_computation.6 | async-start | bytes 9437184 | tf_op jit(solution)/shard_map/psum | solution.py:75
  169.5 0.7 copy-start.2
  270.5 12.6 %copy-start.3 = (f32[1536,768]{1,0:T(8,128)S(1)}, f32[1536,768]{1,0:T(8,128)}, u32[]{:S(2)}) copy-start(f32[1536,768]{1,0:T(8,128)} %all-reduce.2.cloned.1.call-done) | copy-start | bytes 14155780
  270.5 12.6 %copy-start.4 = (bf16[1,1536,768]{2,1,0:T(8,128)(2,1)S(1)}, bf16[1,1536,768]{2,1,0:T(8,128)(2,1)}, u32[]{:S(2)}) copy-start(bf16[1,1536,768]{2,1,0:T(8,128)(2,1)} %param.14) | copy-start | bytes 7077892
  270.5 12.6 %copy-start.5 = (bf16[1,1536,768]{2,1,0:T(8,128)(2,1)S(1)}, bf16[1,1536,768]{2,1,0:T(8,128)(2,1)}, u32[]{:S(2)}) copy-start(bf16[1,1536,768]{2,1,0:T(8,128)(2,1)} %param.13) | copy-start | bytes 7077892
  542.5 18.6 %all-to-all-start.5 = ((f32[8,4,6,1536]{3,0,2,1:T(8,128)}), f32[8,4,6,1536]{3,0,2,1:T(8,128)S(1)}, u32[]{:S(2)}, u32[]{:S(2)}) async-start(f32[8,4,6,1536]{3,0,2,1:T(8,128)} %copy.58), calls=%async_computation.5 | async-start | bytes 2359296 | tf_op jit(solution)/shard_map/all_to_all | solution.py:88
  562.2 4.3 copy-start.1
Sparse Core Ops, SparseCore 0:
  169.6 100.8 all-reduce.1
where the time goes:
time: 575 us; the launch traced here: 573 us
  blocking collectives  376 us (65%)
  waiting for transfers between devices  91.6 us (16%)
  local copies, waits for them, and re-layouts  50.4 us (9%)
  matrix products  32.4 us (6%)
  between operations  13.5 us (2%)
    all_to_all x1, blocking collectives, on_device(): lax.all_to_all(outbound, ('expert', 'etp'), split_axis=0, concat_axis=0,...  218 us
    all_to_all x1, blocking collectives, on_device(): lax.all_to_all(copied, ('expert', 'etp'), split_axis=0, concat_axis=0, ti...  121 us
    psum x1, waiting for transfers between devices, on_device(): hidden_raw = lax.psum(partial_value, 'dp')  76.8 us
    reshape x2, local copies, waits for them, and re-layouts, on_device(): slot_grad.reshape(expert_count * tensor_count, group_count, capacity, qua...  28.4 us
    all_to_all x1, blocking collectives, on_device(): lax.all_to_all(copied_weight, ('expert', 'etp'), split_axis=0, concat_axi...  16.7 us
    all_to_all x1, waiting for transfers between devices, on_device(): lax.all_to_all(inbound, 'dp', split_axis=1, concat_axis=3, tiled=True)  14.8 us
    all_to_all x1, blocking collectives, on_device(): lax.all_to_all(outgoing, 'dp', split_axis=1, concat_axis=1, tiled=True)  13.6 us
    dot_general x1, matrix products, on_device(): jnp.einsum('sf,qf->sq', gate_grad, gate_weight[0], preferred_element_type...  12.6 us
  transfers between devices with their start and end apart: 2, of which 2 were waited for; matrix products, arithmetic and copies ran while one was open for 0% of the time, Pallas kernels for 0%

commit v1 on v0

v1 whole, which is shorter than its diff:
```python
import jax
import jax.numpy as jnp
from jax import lax
from jax.experimental import pallas as pl
from jax.experimental.pallas import tpu as pltpu
from jax.sharding import PartitionSpec as P

MESH = pl.DeviceIdType.MESH
NX, NZ, NT, NY = 4, 8, 8, 4
CAP = 6
ROWS = NX * CAP
BLOCK = 2 * ROWS
META = 128
CHUNKS = ((1, -1), (2, -2), (3, -3), (4, 0))
SKEW = 3
F32, BF16 = jnp.float32, jnp.bfloat16


def dot_nt(a, b):
    return lax.dot_general(a, b, (((1,), (1,)), ((), ())), preferred_element_type=F32)


def aligned(start, unit):
    return pl.multiple_of(start * unit, unit)


def kernel(
    tok, dw_hbm, gw_hbm, uw_hbm, gs_hbm, us_hbm, out,
    dw, gw, uw, gs, us, t2, rows, hp32, hp, xo, xl, xr, hf, gg, ug, sg, yb, pb, yo, yl, yr, zs, zr, fin, fr,
    load_sem, send_sem, recv_sem,
):
    d, e, t = lax.axis_index("dp"), lax.axis_index("expert"), lax.axis_index("etp")
    y, c = lax.div(t, 2), lax.rem(t, 2)
    fh = tok.shape[1] - META
    fq = 2 * fh
    fe = dw.shape[0]
    quarter = 2 * BLOCK

    loads = []
    for i, (src, dst) in enumerate(
        ((dw_hbm, dw), (gs_hbm, gs), (us_hbm, us), (gw_hbm, gw), (uw_hbm, uw))
    ):
        loads.append(pltpu.make_async_copy(src, dst, load_sem.at[i]))
        loads[-1].start()

    def at_x(j):
        return (lax.rem(d + j + NX, NX), e, t)

    def at_y(j):
        return (d, e, 2 * lax.rem(y + j + NY, NY) + c)

    def at_z(j):
        return (d, lax.rem(e + j + NZ, NZ), t)

    sibling = (d, e, 2 * y + 1 - c)

    barrier = pltpu.get_barrier_semaphore()
    partners = [at_x(j) for j in range(1, NX)] + [at_z(j) for j in range(1, NZ)]
    partners += [at_y(1), at_y(-1), sibling]
    for device in partners:
        pl.semaphore_signal(barrier, inc=1, device_id=device, device_id_type=MESH)
    pl.semaphore_wait(barrier, len(partners))

    sent = []

    def send(src, dst, device):
        i = len(sent)
        copy = pltpu.make_async_remote_copy(
            src_ref=src,
            dst_ref=dst,
            send_sem=send_sem.at[i],
            recv_sem=recv_sem.at[i],
            device_id=device,
            device_id_type=MESH,
        )
        copy.start()
        sent.append(copy)
        return copy

    here = pl.ds(aligned(d, 16), 16)
    first = []
    for j in range(1, NX):
        there = pl.ds(aligned(lax.rem(d + j, NX), 16), 16)
        first.append(send(tok.at[there, :], t2.at[0, here, :], at_x(j)))
    t2[0, here, :] = tok[here, :]
    for copy in first:
        copy.wait_recv()
    gather = {
        1: send(t2.at[0], t2.at[1], at_z(-1)),
        -1: send(t2.at[0], t2.at[NZ - 1], at_z(1)),
    }

    def meta_of(r):
        return sum(
            t2[r % NZ, g * 16 : (g + 1) * 16, fh : fh + META].astype(F32) for g in range(NX)
        )

    def meta_row(meta, row):
        ids = lax.broadcasted_iota(jnp.int32, meta.shape, 0)
        return jnp.sum(jnp.where(ids == row, meta, 0.0), axis=0, keepdims=True)[:, :64]

    slot = lax.broadcasted_iota(jnp.int32, (ROWS, 64), 0)
    lane = lax.broadcasted_iota(jnp.int32, (ROWS, 64), 1)
    group = (
        (slot >= CAP).astype(jnp.int32)
        + (slot >= 2 * CAP).astype(jnp.int32)
        + (slot >= 3 * CAP).astype(jnp.int32)
    )
    place = (slot - CAP * group + 1).astype(F32)
    same_group = (lane >> 4) == group
    half_of_lane = (lane >> 3) & 1

    def choose(code, h):
        return same_group & (half_of_lane == h) & (code == place)

    state = [dict() for _ in CHUNKS]

    def select(k):
        for r in CHUNKS[k]:
            if r == 0:
                continue
            gather[r].wait_recv()
            if r > 0 and r < 4:
                gather[r + 1] = send(t2.at[r], t2.at[r + 1], at_z(-1))
            if r < 0 and r > -3:
                gather[r - 1] = send(t2.at[NZ + r], t2.at[NZ + r - 1], at_z(1))
        codes = [meta_row(meta_of(r), e) for r in CHUNKS[k]]
        mine = pl.ds(aligned(t, BLOCK), BLOCK)
        for h in range(2):
            parts = [
                jnp.dot(
                    choose(code, h).astype(F32).astype(BF16),
                    t2[r % NZ, :, 0:fh],
                    preferred_element_type=F32,
                )
                for code, r in zip(codes, CHUNKS[k])
            ]
            rows[k, mine, h * fh : (h + 1) * fh] = jnp.concatenate(parts, axis=0).astype(BF16)
        block = rows.at[k, mine, :]
        state[k]["ag"] = (
            send(block, block, at_y(1)),
            send(block, block, at_y(-1)),
            send(block, block, sibling),
        )

    def gather_pass(k):
        from_left, from_right, other = state[k]["ag"]
        left = pl.ds(aligned(2 * lax.rem(y + NY - 1, NY) + c, BLOCK), BLOCK)
        right = pl.ds(aligned(2 * lax.rem(y + 1, NY) + c, BLOCK), BLOCK)
        from_left.wait_recv()
        half = rows.at[k, left, 0:fh]
        a = send(half, half, at_y(1))
        whole = rows.at[k, left, :]
        sl = send(whole, whole, sibling)
        from_right.wait_recv()
        half = rows.at[k, right, fh:fq]
        b = send(half, half, at_y(-1))
        whole = rows.at[k, right, :]
        sr = send(whole, whole, sibling)
        state[k]["ag2"] = (a, b)
        state[k]["sib"] = [other, sl, sr]

    def gather_last(k):
        opposite = pl.ds(aligned(2 * lax.rem(y + 2, NY) + c, BLOCK), BLOCK)
        a, b = state[k]["ag2"]
        a.wait_recv()
        half = rows.at[k, opposite, 0:fh]
        state[k]["sib"].append(send(half, half, sibling))
        b.wait_recv()
        half = rows.at[k, opposite, fh:fq]
        state[k]["sib"].append(send(half, half, sibling))

    q_right, q_left = lax.rem(d + 1, NX), lax.rem(d + NX - 1, NX)
    q_far = lax.rem(d + 2, NX)

    def half_a(q):
        return pl.ds(pl.multiple_of(q * quarter, quarter), BLOCK)

    def half_b(q):
        return pl.ds(pl.multiple_of(q * quarter + BLOCK, BLOCK), BLOCK)

    def whole_q(q):
        return pl.ds(pl.multiple_of(q * quarter, quarter), quarter)

    def hidden(k):
        for copy in state[k]["sib"]:
            copy.wait_recv()
        if k == 0:
            loads[0].wait()
        tile = min(256, fe)

        @pl.loop(0, fe // tile)
        def _(n):
            cols = pl.ds(pl.multiple_of(n * tile, tile), tile)
            part = dot_nt(rows[k], dw[cols, :])
            hp32[k, :, cols] = part
            hp[k, :, cols] = part.astype(BF16)

        far_a = send(hp.at[k, half_a(q_far), :], xo.at[k, 0], at_x(1))
        far_b = send(hp.at[k, half_b(q_far), :], xo.at[k, 1], at_x(-1))
        near_b = send(hp.at[k, half_b(q_right), :], xl.at[k, BLOCK:quarter, :], at_x(1))
        near_a = send(hp.at[k, half_a(q_left), :], xr.at[k, 0:BLOCK, :], at_x(-1))
        state[k]["rs"] = (far_a, far_b)
        state[k]["rs2"] = [near_b, near_a]

    def reduce_pass(k):
        far_a, far_b = state[k]["rs"]
        far_a.wait_recv()
        to = half_a(q_right)
        hp[k, to, :] = (hp32[k, to, :] + xo[k, 0].astype(F32)).astype(BF16)
        state[k]["rs2"].append(send(hp.at[k, to, :], xl.at[k, 0:BLOCK, :], at_x(1)))
        far_b.wait_recv()
        to = half_b(q_left)
        hp[k, to, :] = (hp32[k, to, :] + xo[k, 1].astype(F32)).astype(BF16)
        state[k]["rs2"].append(send(hp.at[k, to, :], xr.at[k, BLOCK:quarter, :], at_x(-1)))

    def reduce_last(k):
        for copy in state[k]["rs2"]:
            copy.wait_recv()
        mine = whole_q(d)
        total = hp32[k, mine, :] + xl[k].astype(F32) + xr[k].astype(F32)
        hf[k, mine, :] = total.astype(BF16)
        block = hf.at[k, mine, :]
        state[k]["hg"] = (send(block, block, at_x(1)), send(block, block, at_x(-1)))

    def spread_pass(k):
        from_left, from_right = state[k]["hg"]
        from_left.wait_recv()
        block = hf.at[k, half_a(q_left), :]
        a = send(block, block, at_x(1))
        from_right.wait_recv()
        block = hf.at[k, half_b(q_right), :]
        b = send(block, block, at_x(-1))
        state[k]["hg2"] = (a, b)

    def slot_rows(ref, k, cols):
        pieces = []
        for r in CHUNKS[k]:
            source = lax.rem(e + r + NZ, NZ)
            start = pl.multiple_of(source * (NT * ROWS), NT * ROWS)
            pieces.append(ref[pl.ds(start, NT * ROWS), cols].astype(F32))
        return jnp.concatenate(
            [p[i * ROWS : (i + 1) * ROWS] for i in range(NT) for p in pieces], axis=0
        )

    def backward(k):
        for copy in state[k]["hg2"]:
            copy.wait_recv()
        if k == 0:
            for copy in loads[1:]:
                copy.wait()

        @pl.loop(0, fe // 128)
        def _(n):
            cols = pl.ds(pl.multiple_of(n * 128, 128), 128)
            h = hf[k, :, cols].astype(F32)
            gate = slot_rows(gs, k, cols)
            up = slot_rows(us, k, cols)
            s = jax.nn.sigmoid(gate)
            gg[:, cols] = (h * up * s * (1.0 + gate * (1.0 - s))).astype(BF16)
            ug[:, cols] = (h * gate * s).astype(BF16)

        tile = min(256, fq)

        @pl.loop(0, fq // tile)
        def _(n):
            cols = pl.ds(pl.multiple_of(n * tile, tile), tile)
            part = dot_nt(gg[...], gw[cols, :]) + dot_nt(ug[...], uw[cols, :])
            for i in range(NT):
                sg[k, i // 2, i % 2, :, cols] = part[i * BLOCK : (i + 1) * BLOCK]

        state[k]["pair"] = send(sg.at[k, :, 1 - c], yb.at[k], sibling)

    y_right, y_left, y_far = lax.rem(y + 1, NY), lax.rem(y + NY - 1, NY), lax.rem(y + 2, NY)
    low, high = slice(0, fh), slice(fh, fq)

    def pair_sum(k, q, cols):
        return sg[k, q, c, :, cols] + yb[k, q, :, cols]

    def slot_pass(k):
        state[k]["pair"].wait_recv()
        pb[k, 0] = pair_sum(k, y_far, slice(0, fq)).astype(BF16)
        far_a = send(pb.at[k, 0, :, low], yo.at[k, 0], at_y(1))
        far_b = send(pb.at[k, 0, :, high], yo.at[k, 1], at_y(-1))
        pb[k, 1, :, high] = pair_sum(k, y_right, high).astype(BF16)
        near_b = send(pb.at[k, 1, :, high], yl.at[k, :, high], at_y(1))
        pb[k, 2, :, low] = pair_sum(k, y_left, low).astype(BF16)
        near_a = send(pb.at[k, 2, :, low], yr.at[k, :, low], at_y(-1))
        state[k]["ys"] = (far_a, far_b)
        state[k]["ys2"] = [near_b, near_a]

    def slot_pass2(k):
        far_a, far_b = state[k]["ys"]
        far_a.wait_recv()
        pb[k, 1, :, low] = (pair_sum(k, y_right, low) + yo[k, 0].astype(F32)).astype(BF16)
        state[k]["ys2"].append(send(pb.at[k, 1, :, low], yl.at[k, :, low], at_y(1)))
        far_b.wait_recv()
        pb[k, 2, :, high] = (pair_sum(k, y_left, high) + yo[k, 1].astype(F32)).astype(BF16)
        state[k]["ys2"].append(send(pb.at[k, 2, :, high], yr.at[k, :, high], at_y(-1)))

    returns = []

    def slot_last(k):
        for copy in state[k]["ys2"]:
            copy.wait_recv()
        total = pair_sum(k, y, slice(0, fq)) + yl[k].astype(F32) + yr[k].astype(F32)
        for i, r in enumerate(CHUNKS[k]):
            part = total[i * ROWS : (i + 1) * ROWS]
            if r == 0:
                zr[0] = part
            else:
                zs[k, i] = part
                returns.append(send(zs.at[k, i], zr.at[(-r) % NZ], at_z(r)))

    stages = (
        select, gather_pass, gather_last, hidden, reduce_pass, reduce_last,
        spread_pass, backward, slot_pass, slot_pass2, slot_last,
    )
    for step in range(len(stages) + SKEW * (len(CHUNKS) - 1)):
        for k in range(len(CHUNKS)):
            s = step - SKEW * k
            if 0 <= s < len(stages):
                stages[s](k)

    meta = meta_of(0)
    mix = [[], []]
    for j in range(NZ):
        x = lax.rem(e + j, NZ)
        code, weight = meta_row(meta, x), meta_row(meta, x + NZ)
        for h in range(2):
            mix[h].append(jnp.where(choose(code, h), weight, 0.0))
    mix = [jnp.concatenate(m, axis=0).astype(BF16) for m in mix]
    for copy in returns:
        copy.wait_recv()

    def combine(h):
        value = zr[:, :, h * fh : (h + 1) * fh].reshape(NZ * ROWS, fh)
        coarse = value.astype(BF16)
        fine = (value - coarse.astype(F32)).astype(BF16)
        dims = (((0,), (0,)), ((), ()))
        return lax.dot_general(mix[h], coarse, dims, preferred_element_type=F32) + lax.dot_general(
            mix[h], fine, dims, preferred_element_type=F32
        )

    fin[...] = (combine(0) + combine(1)).astype(BF16)
    last = []
    for j in range(1, NX):
        there = pl.ds(aligned(lax.rem(d + j, NX), 16), 16)
        last.append(send(fin.at[there, :], fr.at[here, :], at_x(j)))
    fr[here, :] = fin[here, :]
    for copy in last:
        copy.wait_recv()
    out[...] = fr[...]
    for copy in sent:
        copy.wait_send()


COPIES = 3 + 7 + 4 * (3 + 4 + 2 + 4 + 2 + 2 + 2 + 1 + 4 + 2) + 7 + 3


def on_device(
    grad_output, comb_weights, expert_ids, down_weight, gate_weight, up_weight, gate_saved, up_saved
):
    tokens, width = grad_output.shape
    fq = width // NX
    fh = fq // 2
    fe = down_weight.shape[1]
    slots = gate_saved.shape[1]
    d = lax.axis_index("dp")
    experts = jnp.arange(NZ, dtype=jnp.int32)
    match = expert_ids[None, :, :] == experts[:, None, None]
    hits = jnp.any(match, axis=2)
    earlier = jnp.arange(tokens)[:, None] < jnp.arange(tokens)[None, :]
    before = jnp.sum(jnp.where(hits[:, :, None] & earlier[None], 1.0, 0.0), axis=1)
    code = jnp.where(hits, before + 1.0, 0.0)
    weight = jnp.sum(jnp.where(match, comb_weights.astype(F32)[None], 0.0), axis=2)
    meta = jnp.concatenate([code, weight], axis=0).astype(BF16)
    lanes = jnp.arange(META) // 16 == d
    meta = jnp.where(lanes[None, :], jnp.tile(meta, (1, META // tokens)), 0)
    value = grad_output.reshape(tokens, NX, 2, fh).transpose(1, 2, 0, 3).reshape(NX, 16, fh)
    tok = jnp.concatenate([value, jnp.broadcast_to(meta[None], (NX, 16, META))], axis=2)
    tok = tok.reshape(NX * 16, fh + META)

    n = len(CHUNKS)
    vmem = pltpu.VMEM
    any_space = pl.BlockSpec(memory_space=pl.ANY)
    in_vmem = pl.BlockSpec(memory_space=pltpu.VMEM)
    out = pl.pallas_call(
        kernel,
        out_shape=jax.ShapeDtypeStruct((NX * 16, fh), BF16),
        in_specs=[in_vmem] + [any_space] * 5,
        out_specs=in_vmem,
        scratch_shapes=[
            vmem((fe, fq), BF16),
            vmem((fq, fe), BF16),
            vmem((fq, fe), BF16),
            vmem((slots, fe), BF16),
            vmem((slots, fe), BF16),
            vmem((NZ, 64, fh + META), BF16),
            vmem((n, NT * BLOCK, fq), BF16),
            vmem((n, NT * BLOCK, fe), F32),
            vmem((n, NT * BLOCK, fe), BF16),
            vmem((n, 2, BLOCK, fe), BF16),
            vmem((n, 2 * BLOCK, fe), BF16),
            vmem((n, 2 * BLOCK, fe), BF16),
            vmem((n, NT * BLOCK, fe), BF16),
            vmem((NT * BLOCK, fe), BF16),
            vmem((NT * BLOCK, fe), BF16),
            vmem((n, NY, 2, BLOCK, fq), F32),
            vmem((n, NY, BLOCK, fq), F32),
            vmem((n, 3, BLOCK, fq), BF16),
            vmem((n, 2, BLOCK, fh), BF16),
            vmem((n, BLOCK, fq), BF16),
            vmem((n, BLOCK, fq), BF16),
            vmem((n, 2, ROWS, fq), F32),
            vmem((NZ, ROWS, fq), F32),
            vmem((64, fh), BF16),
            vmem((64, fh), BF16),
            pltpu.SemaphoreType.DMA((5,)),
            pltpu.SemaphoreType.DMA((COPIES,)),
            pltpu.SemaphoreType.DMA((COPIES,)),
        ],
        compiler_params=pltpu.CompilerParams(
            collective_id=0, has_side_effects=True, vmem_limit_bytes=58 * 1024 * 1024
        ),
        cost_estimate=pl.CostEstimate(
            flops=6 * slots * fe * fq, bytes_accessed=12_000_000, transcendentals=slots * fe
        ),
    )(tok, down_weight[0], gate_weight[0], up_weight[0], gate_saved[0], up_saved[0])
    return out.reshape(NX, 2, tokens, fh).transpose(2, 0, 1, 3).reshape(tokens, width)


def solution(mesh):
    in_specs = (
        P(("dp", "expert", "etp"), None),
        P(("dp", "expert", "etp"), None),
        P(("dp", "expert", "etp"), None),
        P("expert", "etp", "dp"),
        P("expert", "dp", "etp"),
        P("expert", "dp", "etp"),
        P("expert", None, "etp"),
        P("expert", None, "etp"),
    )
    return jax.shard_map(
        on_device,
        mesh=mesh,
        in_specs=in_specs,
        out_specs=P(("dp", "expert", "etp"), None),
        check_vma=False,
    )
```

time: 575 us -> 135 us (0.23)
  blocking collectives: 376 us -> 0 us
  Pallas kernels: 0 us -> 130 us
  waiting for transfers between devices: 91.6 us -> 0 us
  local copies, waits for them, and re-layouts: 50.4 us -> 1.69 us
  matrix products: 32.4 us -> 0 us
  between operations: 13.5 us -> 0.04 us
    all_to_all x5 -> x0, blocking collectives: 376 us -> none  [the longest x1 218 us: on_device(): lax.all_to_all(outbound, ('expert', 'etp'), split_axis=0, concat_axis=0,...]
    pallas_call x0 -> x1, Pallas kernels: none -> 130 us  [on_device(): pl.pallas_call(kernel, out_shape=jax.ShapeDtypeStruct((NX * 16, fh), BF16...]
    psum x1 -> x0, waiting for transfers between devices: 76.8 us -> none  [on_device(): hidden_raw = lax.psum(partial_value, 'dp')]
    reshape x6 -> x0, local copies, waits for them, and re-layouts: 37.1 us -> none  [the longest x2 28.4 us: on_device(): slot_grad.reshape(expert_count * tensor_count, group_count, capacity, qua...]
    dot_general x4 -> x0, matrix products: 32.4 us -> none  [the longest x1 12.6 us: on_device(): jnp.einsum('sf,qf->sq', gate_grad, gate_weight[0], preferred_element_type...]
    all_to_all x1 -> x0, waiting for transfers between devices: 14.8 us -> none  [on_device(): lax.all_to_all(inbound, 'dp', split_axis=1, concat_axis=3, tiled=True)]
  transfers between devices with their start and end apart: 2 -> 0, of which waited for: 2 -> 0; matrix products, arithmetic and copies ran while one was open for 0% -> 0% of each run, Pallas kernels for 0% -> 0%
where the time goes in v1:
time: 135 us
  Pallas kernels  130 us (96%)
  other arithmetic  3.83 us (3%)
  local copies, waits for them, and re-layouts  1.69 us (1%)
    pallas_call x1, Pallas kernels, on_device(): pl.pallas_call(kernel, out_shape=jax.ShapeDtypeStruct((NX * 16, fh), BF16...  130 us

profile of v1, /device:TPU:1, one launch (start us, length us, event | category | flops | bytes accessed | tf_op | source)
XLA Modules:
  0.0 135.1 jit_solution(1467294687175897444)
XLA Ops:
  0.0 0.7 fusion
  0.7 0.7 convert_element_type.10
  1.4 0.7 select_reduce_fusion.1
  2.1 0.1 select_reduce_fusion
  2.2 0.1 copy.15
  2.3 0.1 bitcast_select_fusion
  2.4 0.1 copy.16
  2.4 1.6 %pad_maximum_fusion.tok = bf16[64,896]{1,0:T(8,128)(2,1)} fusion(bf16[64,128]{1,0:T(8,128)(2,1)S(1)} %bitcast.20, bf16[64,768]{1,0:T(8,128)(2,1)} %bitcast.18), kind=kLoop, calls=%fused_computation | loop fusion | flops 229376 | bytes 229376 | tf_op jit(solution)/shard_map/concatenate | solution.py:381
  4.0 129.5 %shard_map.82 = bf16[64,768]{1,0:T(8,128)(2,1)} custom-call(bf16[64,896]{1,0:T(8,128)(2,1)} %pad_maximum_fusion.tok, bf16[768,1536]{1,0:T(8,128)(2,1)} %bitcast.21, bf16[1536,768]{1,0:T(8,128)(2,1)} %bitcast.22, bf16[1536,768]{1,0:T(8,128)(2,1)} %bitcast.23, bf16[1536,768]{1,0:T(8,128)(2,1)} %bitcast.24, bf16[1536,768]{1,0:T(8,128)(2,1)} %bitcast.25), custom_call_target="tpu_custom_call" | custom-call | flops 10871635968 | bytes 12000000 | tf_op jit(solution)/shard_map/pallas_call | solution.py:388
  133.5 1.5 %copy.18 = bf16[8,6144]{1,0:T(8,128)(2,1)} copy(bf16[8,6144]{1,0:T(8,128)(2,1)} %bitcast.19) | data formatting | bytes 196608
  (5 shorter events, 0.0 us)

commit v2 on v1

v2 whole, which is shorter than its diff:
```python
import jax
import jax.numpy as jnp
from jax import lax
from jax.experimental import pallas as pl
from jax.experimental.pallas import tpu as pltpu
from jax.sharding import PartitionSpec as P

MESH = pl.DeviceIdType.MESH
NX, NZ, NT, NY = 4, 8, 8, 4
CAP = 6
ROWS = NX * CAP
META = 128
CHUNKS = (0, 1, -2, 3, 4, -3, 2, -1)
ORDER = (
    ("d1", 0), ("select", 0), ("z0", 0), ("gr", 0), ("gl", 0), ("select", 7), ("zf", -1),
    ("zf", 1), ("select", 1), ("ga", 0), ("hidden", 0), ("gr", 7), ("gl", 7), ("zf", -2),
    ("zf", 2), ("select", 2), ("select", 6), ("ga", 7), ("rb", 0), ("ra", 0), ("gl", 1),
    ("gr", 1), ("hidden", 7), ("ga", 1), ("select", 5), ("zf", 3), ("select", 3), ("rl", 0),
    ("gr", 2), ("gl", 2), ("hidden", 1), ("rb", 7), ("ra", 7), ("ga", 2), ("gl", 6), ("gr", 6),
    ("hidden", 2), ("select", 4), ("ga", 6), ("rb", 1), ("ra", 1), ("sb", 0), ("sa", 0),
    ("gl", 5), ("gr", 5), ("rl", 7), ("hidden", 6), ("rb", 2), ("ra", 2), ("ga", 5), ("rl", 1),
    ("gl", 3), ("gr", 3), ("hidden", 5), ("back", 0), ("ga", 3), ("rb", 6), ("gr", 4), ("ra", 6),
    ("gl", 4), ("rl", 2), ("sb", 7), ("sa", 7), ("ga", 4), ("sa", 1), ("sb", 1), ("sp", 0),
    ("rb", 5), ("ra", 5), ("hidden", 3), ("hidden", 4), ("rl", 6), ("sb", 2), ("sa", 2),
    ("back", 7), ("rl", 5), ("rb", 3), ("sl", 0), ("ra", 3), ("back", 1), ("rb", 4), ("sp", 7),
    ("ra", 4), ("sa", 6), ("sb", 6), ("back", 2), ("rl", 3), ("sp", 1), ("sb", 5), ("sa", 5),
    ("rl", 4), ("back", 6), ("sp", 2), ("sl", 7), ("sb", 3), ("sa", 3), ("back", 5), ("sp", 6),
    ("sl", 1), ("sb", 4), ("back", 3), ("sp", 5), ("sl", 2), ("sa", 4), ("sp", 3), ("sl", 6),
    ("back", 4), ("sl", 5), ("sp", 4), ("sl", 3), ("sl", 4), ("end", 0), ("fin", 0),
)
F32, BF16 = jnp.float32, jnp.bfloat16


def dot_nt(a, b):
    return lax.dot_general(a, b, (((1,), (1,)), ((), ())), preferred_element_type=F32)


def aligned(start, unit):
    return pl.multiple_of(start * unit, unit)


def kernel(
    tok, dw_hbm, gw_hbm, uw_hbm, gs_hbm, us_hbm, out,
    dw, gw, uw, gs, us, t2, rows, lhs, hp32, hp, xo, xl, xr, hf, gg, ug, sg, yb, pb, yr, zs, zr, fin, fr,
    load_sem, send_sem, recv_sem,
):
    d, e, t = lax.axis_index("dp"), lax.axis_index("expert"), lax.axis_index("etp")
    y, c = lax.div(t, 2), lax.rem(t, 2)
    fh = tok.shape[1] - META
    fq = 2 * fh
    fe = dw.shape[0]

    loads = []
    for i, (src, dst) in enumerate(
        ((dw_hbm, dw), (gs_hbm, gs), (us_hbm, us), (gw_hbm, gw), (uw_hbm, uw))
    ):
        loads.append(pltpu.make_async_copy(src, dst, load_sem.at[i]))
        loads[-1].start()

    def at_x(j):
        return (lax.rem(d + j + NX, NX), e, t)

    def at_y(j):
        return (d, e, 2 * lax.rem(y + j + NY, NY) + c)

    def at_z(j):
        return (d, lax.rem(e + j + NZ, NZ), t)

    sibling = (d, e, 2 * y + 1 - c)

    barrier = pltpu.get_barrier_semaphore()
    partners = [at_x(j) for j in range(1, NX)] + [at_z(j) for j in range(1, NZ)]
    partners += [at_y(j) for j in range(1, NY)] + [sibling]
    for device in partners:
        pl.semaphore_signal(barrier, inc=1, device_id=device, device_id_type=MESH)
    pl.semaphore_wait(barrier, len(partners))

    sent = []

    def send(src, dst, device):
        i = len(sent)
        copy = pltpu.make_async_remote_copy(
            src_ref=src,
            dst_ref=dst,
            send_sem=send_sem.at[i],
            recv_sem=recv_sem.at[i],
            device_id=device,
            device_id_type=MESH,
        )
        copy.start()
        sent.append(copy)
        return copy

    here = pl.ds(aligned(d, 16), 16)
    first, gather, returns, last = [], {}, [], []
    state = [dict() for _ in CHUNKS]
    seen = []

    def arrived(copy):
        if not any(copy is other for other in seen):
            seen.append(copy)
            copy.wait_recv()

    def d1(_):
        for j in range(1, NX):
            there = pl.ds(aligned(lax.rem(d + j, NX), 16), 16)
            first.append(send(tok.at[there, :], t2.at[0, here, :], at_x(j)))
        t2[0, here, :] = tok[here, :]

    def z0(_):
        for copy in first:
            arrived(copy)
        gather[1] = send(t2.at[0], t2.at[1], at_z(-1))
        gather[-1] = send(t2.at[0], t2.at[NZ - 1], at_z(1))

    def zf(r):
        arrived(gather[r])
        if r > 0:
            gather[r + 1] = send(t2.at[r], t2.at[r + 1], at_z(-1))
        else:
            gather[r - 1] = send(t2.at[NZ + r], t2.at[NZ + r - 1], at_z(1))

    def meta_of(r):
        return sum(
            t2[r % NZ, g * 16 : (g + 1) * 16, fh : fh + META].astype(F32) for g in range(NX)
        )

    def meta_row(meta, row):
        ids = lax.broadcasted_iota(jnp.int32, meta.shape, 0)
        return jnp.sum(jnp.where(ids == row, meta, 0.0), axis=0, keepdims=True)[:, :64]

    slot = lax.broadcasted_iota(jnp.int32, (ROWS, 64), 0)
    lane = lax.broadcasted_iota(jnp.int32, (ROWS, 64), 1)
    group = (
        (slot >= CAP).astype(jnp.int32)
        + (slot >= 2 * CAP).astype(jnp.int32)
        + (slot >= 3 * CAP).astype(jnp.int32)
    )
    place = (slot - CAP * group + 1).astype(F32)
    same_group = (lane >> 4) == group
    half_of_lane = (lane >> 3) & 1

    def choose(code, h):
        return same_group & (half_of_lane == h) & (code == place)

    t_left = 2 * lax.rem(y + NY - 1, NY) + c
    t_right = 2 * lax.rem(y + 1, NY) + c
    t_far = 2 * lax.rem(y + 2, NY) + c

    def select(k):
        r = CHUNKS[k]
        for copy in first if r == 0 else (gather[r],):
            arrived(copy)
        code = meta_row(meta_of(r), e)
        for h in range(2):
            part = jnp.dot(
                choose(code, h).astype(F32).astype(BF16),
                t2[r % NZ, :, 0:fh],
                preferred_element_type=F32,
            )
            rows[k, t, :, h * fh : (h + 1) * fh] = part.astype(BF16)
        block = rows.at[k, t]
        state[k]["ag"] = [send(block, block, device) for device in (at_y(1), at_y(-1), at_y(2))]
        state[k]["sib"] = [send(block, block, sibling)]

    def pass_on(k, i, there):
        state[k]["ag"][i].wait_recv()
        block = rows.at[k, there]
        state[k]["sib"].append(send(block, block, sibling))

    def gl(k):
        pass_on(k, 0, t_left)

    def gr(k):
        pass_on(k, 1, t_right)

    def ga(k):
        pass_on(k, 2, t_far)

    q_right, q_left = lax.rem(d + 1, NX), lax.rem(d + NX - 1, NX)
    q_far = lax.rem(d + 2, NX)
    half_a, half_b = slice(0, fe // 2), slice(fe // 2, fe)

    def quarter(q):
        return pl.ds(aligned(q, 2 * ROWS), 2 * ROWS)

    def hidden(k):
        for copy in state[k]["sib"]:
            copy.wait_recv()
        if loads[0] is not None:
            loads[0].wait()
            loads[0] = None
        lhs[...] = rows[k].astype(F32).reshape(NT * ROWS, fq).astype(BF16)
        tile = min(256, fe)

        @pl.loop(0, fe // tile)
        def _(n):
            cols = pl.ds(pl.multiple_of(n * tile, tile), tile)
            part = dot_nt(lhs[...], dw[cols, :])
            hp32[k, :, cols] = part
            hp[k, :, cols] = part.astype(BF16)

        far, right, left = quarter(q_far), quarter(q_right), quarter(q_left)
        far_a = send(hp.at[k, far, half_a], xo.at[k, :, half_a], at_x(1))
        far_b = send(hp.at[k, far, half_b], xo.at[k, :, half_b], at_x(-1))
        near_b = send(hp.at[k, right, half_b], xl.at[k, :, half_b], at_x(1))
        near_a = send(hp.at[k, left, half_a], xr.at[k, :, half_a], at_x(-1))
        state[k]["rs"] = (far_a, far_b)
        state[k]["rs2"] = [near_b, near_a]

    def add_far(k, i, to, half, dst, device):
        state[k]["rs"][i].wait_recv()
        hp[k, to, half] = (hp32[k, to, half] + xo[k, :, half].astype(F32)).astype(BF16)
        state[k]["rs2"].append(send(hp.at[k, to, half], dst.at[k, :, half], device))

    def ra(k):
        add_far(k, 0, quarter(q_right), half_a, xl, at_x(1))

    def rb(k):
        add_far(k, 1, quarter(q_left), half_b, xr, at_x(-1))

    def rl(k):
        for copy in state[k]["rs2"]:
            copy.wait_recv()
        mine = quarter(d)
        total = hp32[k, mine, :] + xl[k].astype(F32) + xr[k].astype(F32)
        hf[k, mine, :] = total.astype(BF16)
        block = hf.at[k, mine, :]
        state[k]["hg"] = (send(block, block, at_x(1)), send(block, block, at_x(-1)))
        state[k]["hg2"] = []

    def sa(k):
        state[k]["hg"][0].wait_recv()
        block = hf.at[k, quarter(q_left), half_a]
        state[k]["hg2"].append(send(block, block, at_x(1)))

    def sb(k):
        state[k]["hg"][1].wait_recv()
        block = hf.at[k, quarter(q_right), half_b]
        state[k]["hg2"].append(send(block, block, at_x(-1)))

    def back(k):
        for copy in state[k]["hg2"]:
            copy.wait_recv()
        while len(loads) > 1:
            loads.pop().wait()
        source = lax.rem(e + CHUNKS[k] + NZ, NZ)
        slots = pl.ds(aligned(source, NT * ROWS), NT * ROWS)

        @pl.loop(0, fe // 128)
        def _(n):
            cols = pl.ds(pl.multiple_of(n * 128, 128), 128)
            h = hf[k, :, cols].astype(F32)
            gate = gs[slots, cols].astype(F32)
            up = us[slots, cols].astype(F32)
            s = jax.nn.sigmoid(gate)
            gg[:, cols] = (h * up * s * (1.0 + gate * (1.0 - s))).astype(BF16)
            ug[:, cols] = (h * gate * s).astype(BF16)

        tile = 512 if fq % 512 == 0 else min(256, fq)

        @pl.loop(0, fq // tile)
        def _(n):
            cols = pl.ds(pl.multiple_of(n * tile, tile), tile)
            part = dot_nt(gg[...], gw[cols, :]) + dot_nt(ug[...], uw[cols, :])
            for i in range(NT):
                sg[k, i // 2, i % 2, :, cols] = part[i * ROWS : (i + 1) * ROWS]

        state[k]["pair"] = send(sg.at[k, :, 1 - c], yb.at[k], sibling)

    def sp(k):
        state[k]["pair"].wait_recv()
        state[k]["ys"] = []
        for i in range(1, NY):
            q = lax.rem(y + i, NY)
            pb[k, i - 1] = (sg[k, q, c] + yb[k, q]).astype(BF16)
            state[k]["ys"].append(send(pb.at[k, i - 1], yr.at[k, i - 1], at_y(i)))

    def sl(k):
        for copy in state[k]["ys"]:
            copy.wait_recv()
        total = sg[k, y, c] + yb[k, y]
        for i in range(NY - 1):
            total = total + yr[k, i].astype(F32)
        r = CHUNKS[k]
        if r == 0:
            zr[0] = total
        else:
            zs[k] = total
            returns.append(send(zs.at[k], zr.at[(-r) % NZ], at_z(r)))

    def end(_):
        meta = meta_of(0)
        mix = [[], []]
        for j in range(NZ):
            x = lax.rem(e + j, NZ)
            code, weight = meta_row(meta, x), meta_row(meta, x + NZ)
            for h in range(2):
                mix[h].append(jnp.where(choose(code, h), weight, 0.0))
        mix = [jnp.concatenate(m, axis=0).astype(BF16) for m in mix]
        for copy in returns:
            copy.wait_recv()

        def combine(h):
            value = zr[:, :, h * fh : (h + 1) * fh].reshape(NZ * ROWS, fh)
            coarse = value.astype(BF16)
            fine = (value - coarse.astype(F32)).astype(BF16)
            dims = (((0,), (0,)), ((), ()))
            return lax.dot_general(mix[h], coarse, dims, preferred_element_type=F32) + lax.dot_general(
                mix[h], fine, dims, preferred_element_type=F32
            )

        fin[...] = (combine(0) + combine(1)).astype(BF16)
        for j in range(1, NX):
            there = pl.ds(aligned(lax.rem(d + j, NX), 16), 16)
            last.append(send(fin.at[there, :], fr.at[here, :], at_x(j)))
        fr[here, :] = fin[here, :]

    def finish(_):
        for copy in last:
            copy.wait_recv()
        out[...] = fr[...]

    stages = {
        "d1": d1, "z0": z0, "zf": zf, "select": select, "gl": gl, "gr": gr, "ga": ga,
        "hidden": hidden, "ra": ra, "rb": rb, "rl": rl, "sa": sa, "sb": sb,
        "back": back, "sp": sp, "sl": sl, "end": end, "fin": finish,
    }
    for name, k in ORDER:
        stages[name](k)
    for copy in sent:
        copy.wait_send()


COPIES = 3 + 7 + 8 * (4 + 3 + 4 + 2 + 2 + 2 + 1 + 3) + 7 + 3


def on_device(
    grad_output, comb_weights, expert_ids, down_weight, gate_weight, up_weight, gate_saved, up_saved
):
    tokens, width = grad_output.shape
    fq = width // NX
    fh = fq // 2
    fe = down_weight.shape[1]
    slots = gate_saved.shape[1]
    d = lax.axis_index("dp")
    experts = jnp.arange(NZ, dtype=jnp.int32)
    match = expert_ids[None, :, :] == experts[:, None, None]
    hits = jnp.any(match, axis=2)
    earlier = jnp.arange(tokens)[:, None] < jnp.arange(tokens)[None, :]
    before = jnp.sum(jnp.where(hits[:, :, None] & earlier[None], 1.0, 0.0), axis=1)
    code = jnp.where(hits, before + 1.0, 0.0)
    weight = jnp.sum(jnp.where(match, comb_weights.astype(F32)[None], 0.0), axis=2)
    meta = jnp.concatenate([code, weight], axis=0).astype(BF16)
    lanes = jnp.arange(META) // 16 == d
    meta = jnp.where(lanes[None, :], jnp.tile(meta, (1, META // tokens)), 0)
    value = grad_output.reshape(tokens, NX, 2, fh).transpose(1, 2, 0, 3).reshape(NX, 16, fh)
    tok = jnp.concatenate([value, jnp.broadcast_to(meta[None], (NX, 16, META))], axis=2)
    tok = tok.reshape(NX * 16, fh + META)

    n = len(CHUNKS)
    vmem = pltpu.VMEM
    any_space = pl.BlockSpec(memory_space=pl.ANY)
    in_vmem = pl.BlockSpec(memory_space=pltpu.VMEM)
    out = pl.pallas_call(
        kernel,
        out_shape=jax.ShapeDtypeStruct((NX * 16, fh), BF16),
        in_specs=[in_vmem] + [any_space] * 5,
        out_specs=in_vmem,
        scratch_shapes=[
            vmem((fe, fq), BF16),
            vmem((fq, fe), BF16),
            vmem((fq, fe), BF16),
            vmem((slots, fe), BF16),
            vmem((slots, fe), BF16),
            vmem((NZ, 64, fh + META), BF16),
            vmem((n, NT, ROWS, fq), BF16),
            vmem((NT * ROWS, fq), BF16),
            vmem((n, NT * ROWS, fe), F32),
            vmem((n, NT * ROWS, fe), BF16),
            vmem((n, 2 * ROWS, fe), BF16),
            vmem((n, 2 * ROWS, fe), BF16),
            vmem((n, 2 * ROWS, fe), BF16),
            vmem((n, NT * ROWS, fe), BF16),
            vmem((NT * ROWS, fe), BF16),
            vmem((NT * ROWS, fe), BF16),
            vmem((n, NY, 2, ROWS, fq), F32),
            vmem((n, NY, ROWS, fq), F32),
            vmem((n, NY - 1, ROWS, fq), BF16),
            vmem((n, NY - 1, ROWS, fq), BF16),
            vmem((n, ROWS, fq), F32),
            vmem((NZ, ROWS, fq), F32),
            vmem((64, fh), BF16),
            vmem((64, fh), BF16),
            pltpu.SemaphoreType.DMA((5,)),
            pltpu.SemaphoreType.DMA((COPIES,)),
            pltpu.SemaphoreType.DMA((COPIES,)),
        ],
        compiler_params=pltpu.CompilerParams(
            collective_id=0, has_side_effects=True, vmem_limit_bytes=58 * 1024 * 1024
        ),
        cost_estimate=pl.CostEstimate(
            flops=6 * slots * fe * fq, bytes_accessed=12_000_000, transcendentals=slots * fe
        ),
    )(tok, down_weight[0], gate_weight[0], up_weight[0], gate_saved[0], up_saved[0])
    return out.reshape(NX, 2, tokens, fh).transpose(2, 0, 1, 3).reshape(tokens, width)


def solution(mesh):
    in_specs = (
        P(("dp", "expert", "etp"), None),
        P(("dp", "expert", "etp"), None),
        P(("dp", "expert", "etp"), None),
        P("expert", "etp", "dp"),
        P("expert", "dp", "etp"),
        P("expert", "dp", "etp"),
        P("expert", None, "etp"),
        P("expert", None, "etp"),
    )
    return jax.shard_map(
        on_device,
        mesh=mesh,
        in_specs=in_specs,
        out_specs=P(("dp", "expert", "etp"), None),
        check_vma=False,
    )
```

time: 135 us -> 112 us (0.83)
  Pallas kernels: 130 us -> 106 us
    pallas_call x1, Pallas kernels: 130 us -> 106 us  [on_device(): pl.pallas_call(kernel, out_shape=jax.ShapeDtypeStruct((NX * 16, fh), BF16...]
where the time goes in v2:
time: 112 us
  Pallas kernels  106 us (95%)
  other arithmetic  3.83 us (3%)
  local copies, waits for them, and re-layouts  1.69 us (2%)
    pallas_call x1, Pallas kernels, on_device(): pl.pallas_call(kernel, out_shape=jax.ShapeDtypeStruct((NX * 16, fh), BF16...  106 us

profile of v2, /device:TPU:1, one launch (start us, length us, event | category | flops | bytes accessed | tf_op | source)
XLA Modules:
  0.0 112.0 jit_solution(12181017246181783842)
XLA Ops:
  0.0 0.7 fusion
  0.7 0.7 convert_element_type.10
  1.4 0.7 select_reduce_fusion.1
  2.1 0.1 select_reduce_fusion
  2.2 0.1 copy.15
  2.3 0.1 bitcast_select_fusion
  2.4 0.1 copy.16
  2.4 1.6 %pad_maximum_fusion.tok = bf16[64,896]{1,0:T(8,128)(2,1)} fusion(bf16[64,128]{1,0:T(8,128)(2,1)S(1)} %bitcast.20, bf16[64,768]{1,0:T(8,128)(2,1)} %bitcast.18), kind=kLoop, calls=%fused_computation | loop fusion | flops 229376 | bytes 229376 | tf_op jit(solution)/shard_map/concatenate | solution.py:358
  4.0 106.4 %shard_map.82 = bf16[64,768]{1,0:T(8,128)(2,1)} custom-call(bf16[64,896]{1,0:T(8,128)(2,1)} %pad_maximum_fusion.tok, bf16[768,1536]{1,0:T(8,128)(2,1)} %bitcast.21, bf16[1536,768]{1,0:T(8,128)(2,1)} %bitcast.22, bf16[1536,768]{1,0:T(8,128)(2,1)} %bitcast.23, bf16[1536,768]{1,0:T(8,128)(2,1)} %bitcast.24, bf16[1536,768]{1,0:T(8,128)(2,1)} %bitcast.25), custom_call_target="tpu_custom_call" | custom-call | flops 10871635968 | bytes 12000000 | tf_op jit(solution)/shard_map/pallas_call | solution.py:365
  110.5 1.5 %copy.18 = bf16[8,6144]{1,0:T(8,128)(2,1)} copy(bf16[8,6144]{1,0:T(8,128)(2,1)} %bitcast.19) | data formatting | bytes 196608
  (5 shorter events, 0.0 us)

commit v3 on v2

--- a/solution.py
+++ b/solution.py
@@ -40,14 +40,14 @@
 
 
 def kernel(
-    tok, dw_hbm, gw_hbm, uw_hbm, gs_hbm, us_hbm, out,
-    dw, gw, uw, gs, us, t2, rows, lhs, hp32, hp, xo, xl, xr, hf, gg, ug, sg, yb, pb, yr, zs, zr, fin, fr,
+    grad, ids, comb, dw_hbm, gw_hbm, uw_hbm, gs_hbm, us_hbm, out,
+    dw, gw, uw, gs, us, tok, t2, rows, lhs, hp32, hp, xo, xl, xr, hf, gg, ug, sg, yb, pb, yr, zs, zr, fin, fr,
     load_sem, send_sem, recv_sem,
 ):
     d, e, t = lax.axis_index("dp"), lax.axis_index("expert"), lax.axis_index("etp")
     y, c = lax.div(t, 2), lax.rem(t, 2)
-    fh = tok.shape[1] - META
-    fq = 2 * fh
+    fq = grad.shape[1] // NX
+    fh = fq // 2
     fe = dw.shape[0]
 
     loads = []
@@ -73,6 +73,31 @@
     partners += [at_y(j) for j in range(1, NY)] + [sibling]
     for device in partners:
         pl.semaphore_signal(barrier, inc=1, device_id=device, device_id_type=MESH)
+
+    tokens = grad.shape[0]
+    experts = lax.broadcasted_iota(jnp.int32, (NZ, tokens), 0)
+    choices = [ids[i : i + 1, :] == experts for i in range(ids.shape[0])]
+    hits = sum(jnp.where(m, 1.0, 0.0) for m in choices)
+    weight = sum(
+        jnp.where(m, comb[i : i + 1, :].astype(F32), 0.0) for i, m in enumerate(choices)
+    )
+    earlier = lax.broadcasted_iota(jnp.int32, (tokens, tokens), 0) < lax.broadcasted_iota(
+        jnp.int32, (tokens, tokens), 1
+    )
+    before = jnp.dot(
+        hits.astype(BF16), jnp.where(earlier, 1.0, 0.0).astype(BF16), preferred_element_type=F32
+    )
+    code = jnp.where(hits > 0.0, before + 1.0, 0.0)
+    lanes = lax.broadcasted_iota(jnp.int32, (tokens, META), 1)
+    token = lax.broadcasted_iota(jnp.int32, (tokens, META), 0)
+    spread = jnp.where(((lanes >> 4) == d) & ((lanes & 7) == token), 1.0, 0.0).astype(BF16)
+    meta_here = jnp.dot(
+        jnp.concatenate([code, weight], axis=0).astype(BF16), spread, preferred_element_type=F32
+    ).astype(BF16)
+    for q in range(NX):
+        parts = [grad[:, (2 * q + h) * fh : (2 * q + h + 1) * fh].astype(F32) for h in range(2)]
+        tok[q * 16 : (q + 1) * 16, 0:fh] = jnp.concatenate(parts, axis=0).astype(BF16)
+        tok[q * 16 : (q + 1) * 16, fh : fh + META] = meta_here
     pl.semaphore_wait(barrier, len(partners))
 
     sent = []
@@ -319,7 +344,11 @@
     def finish(_):
         for copy in last:
             copy.wait_recv()
-        out[...] = fr[...]
+        for q in range(NX):
+            both = fr[q * 16 : (q + 1) * 16, :].astype(F32)
+            for h in range(2):
+                cols = slice((2 * q + h) * fh, (2 * q + h + 1) * fh)
+                out[:, cols] = both[h * tokens : (h + 1) * tokens].astype(BF16)
 
     stages = {
         "d1": d1, "z0": z0, "zf": zf, "select": select, "gl": gl, "gr": gr, "ga": ga,
@@ -343,29 +372,14 @@
     fh = fq // 2
     fe = down_weight.shape[1]
     slots = gate_saved.shape[1]
-    d = lax.axis_index("dp")
-    experts = jnp.arange(NZ, dtype=jnp.int32)
-    match = expert_ids[None, :, :] == experts[:, None, None]
-    hits = jnp.any(match, axis=2)
-    earlier = jnp.arange(tokens)[:, None] < jnp.arange(tokens)[None, :]
-    before = jnp.sum(jnp.where(hits[:, :, None] & earlier[None], 1.0, 0.0), axis=1)
-    code = jnp.where(hits, before + 1.0, 0.0)
-    weight = jnp.sum(jnp.where(match, comb_weights.astype(F32)[None], 0.0), axis=2)
-    meta = jnp.concatenate([code, weight], axis=0).astype(BF16)
-    lanes = jnp.arange(META) // 16 == d
-    meta = jnp.where(lanes[None, :], jnp.tile(meta, (1, META // tokens)), 0)
-    value = grad_output.reshape(tokens, NX, 2, fh).transpose(1, 2, 0, 3).reshape(NX, 16, fh)
-    tok = jnp.concatenate([value, jnp.broadcast_to(meta[None], (NX, 16, META))], axis=2)
-    tok = tok.reshape(NX * 16, fh + META)
-
     n = len(CHUNKS)
     vmem = pltpu.VMEM
     any_space = pl.BlockSpec(memory_space=pl.ANY)
     in_vmem = pl.BlockSpec(memory_space=pltpu.VMEM)
-    out = pl.pallas_call(
+    return pl.pallas_call(
         kernel,
-        out_shape=jax.ShapeDtypeStruct((NX * 16, fh), BF16),
-        in_specs=[in_vmem] + [any_space] * 5,
+        out_shape=jax.ShapeDtypeStruct((tokens, width), BF16),
+        in_specs=[in_vmem] * 3 + [any_space] * 5,
         out_specs=in_vmem,
         scratch_shapes=[
             vmem((fe, fq), BF16),
@@ -373,6 +387,7 @@
             vmem((fq, fe), BF16),
             vmem((slots, fe), BF16),
             vmem((slots, fe), BF16),
+            vmem((NX * 16, fh + META), BF16),
             vmem((NZ, 64, fh + META), BF16),
             vmem((n, NT, ROWS, fq), BF16),
             vmem((NT * ROWS, fq), BF16),
@@ -402,8 +417,10 @@
         cost_estimate=pl.CostEstimate(
             flops=6 * slots * fe * fq, bytes_accessed=12_000_000, transcendentals=slots * fe
         ),
-    )(tok, down_weight[0], gate_weight[0], up_weight[0], gate_saved[0], up_saved[0])
-    return out.reshape(NX, 2, tokens, fh).transpose(2, 0, 1, 3).reshape(tokens, width)
+    )(
+        grad_output, expert_ids.T, comb_weights.T,
+        down_weight[0], gate_weight[0], up_weight[0], gate_saved[0], up_saved[0],
+    )
 
 
 def solution(mesh):

time: 112 us -> 108 us (0.964)
  other arithmetic: 3.83 us -> 0 us
    concatenate x2 -> x0, other arithmetic: 1.57 us -> none  [the longest x1 1.56 us: on_device(): jnp.concatenate([value, jnp.broadcast_to(meta[None], (NX, 16, META))], ax...]
where the time goes in v3:
time: 108 us
  Pallas kernels  106 us (98%)
  local copies, waits for them, and re-layouts  1.54 us (1%)
    pallas_call x1, Pallas kernels, on_device(): pl.pallas_call(kernel, out_shape=jax.ShapeDtypeStruct((tokens, width), BF...  106 us

profile of v3, /device:TPU:1, one launch (start us, length us, event | category | flops | bytes accessed | tf_op | source)
XLA Modules:
  0.0 108.0 jit_solution(3706068691016156236)
XLA Ops:
  0.0 106.4 %shard_map.82 = bf16[8,6144]{1,0:T(8,128)(2,1)} custom-call(bf16[8,6144]{1,0:T(8,128)(2,1)} %grad.1, s32[4,8]{1,0:T(4,128)} %bitcast.12, bf16[4,8]{1,0:T(4,128)(2,1)} %bitcast.13, bf16[768,1536]{1,0:T(8,128)(2,1)} %bitcast.7, bf16[1536,768]{1,0:T(8,128)(2,1)} %bitcast.8, bf16[1536,768]{1,0:T(8,128)(2,1)} %bitcast.9, bf16[1536,768]{1,0:T(8,128)(2,1)} %bitcast.10, ...), custom_call_target="tpu_custom_call" | custom-call | flops 10871635968 | bytes 12000000 | tf_op jit(solution)/shard_map/pallas_call | solution.py:379
  106.4 1.5 %copy.10 = bf16[8,6144]{1,0:T(8,128)(2,1)} copy(bf16[8,6144]{1,0:T(8,128)(2,1)} %shard_map.82) | data formatting | bytes 196608

commit v4 on v3

--- a/solution.py
+++ b/solution.py
@@ -10,23 +10,24 @@
 CAP = 6
 ROWS = NX * CAP
 META = 128
+FAR = 3
 CHUNKS = (0, 1, -2, 3, 4, -3, 2, -1)
 ORDER = (
-    ("d1", 0), ("select", 0), ("z0", 0), ("gr", 0), ("gl", 0), ("select", 7), ("zf", -1),
-    ("zf", 1), ("select", 1), ("ga", 0), ("hidden", 0), ("gr", 7), ("gl", 7), ("zf", -2),
-    ("zf", 2), ("select", 2), ("select", 6), ("ga", 7), ("rb", 0), ("ra", 0), ("gl", 1),
-    ("gr", 1), ("hidden", 7), ("ga", 1), ("select", 5), ("zf", 3), ("select", 3), ("rl", 0),
-    ("gr", 2), ("gl", 2), ("hidden", 1), ("rb", 7), ("ra", 7), ("ga", 2), ("gl", 6), ("gr", 6),
-    ("hidden", 2), ("select", 4), ("ga", 6), ("rb", 1), ("ra", 1), ("sb", 0), ("sa", 0),
-    ("gl", 5), ("gr", 5), ("rl", 7), ("hidden", 6), ("rb", 2), ("ra", 2), ("ga", 5), ("rl", 1),
-    ("gl", 3), ("gr", 3), ("hidden", 5), ("back", 0), ("ga", 3), ("rb", 6), ("gr", 4), ("ra", 6),
-    ("gl", 4), ("rl", 2), ("sb", 7), ("sa", 7), ("ga", 4), ("sa", 1), ("sb", 1), ("sp", 0),
-    ("rb", 5), ("ra", 5), ("hidden", 3), ("hidden", 4), ("rl", 6), ("sb", 2), ("sa", 2),
-    ("back", 7), ("rl", 5), ("rb", 3), ("sl", 0), ("ra", 3), ("back", 1), ("rb", 4), ("sp", 7),
-    ("ra", 4), ("sa", 6), ("sb", 6), ("back", 2), ("rl", 3), ("sp", 1), ("sb", 5), ("sa", 5),
-    ("rl", 4), ("back", 6), ("sp", 2), ("sl", 7), ("sb", 3), ("sa", 3), ("back", 5), ("sp", 6),
-    ("sl", 1), ("sb", 4), ("back", 3), ("sp", 5), ("sl", 2), ("sa", 4), ("sp", 3), ("sl", 6),
-    ("back", 4), ("sl", 5), ("sp", 4), ("sl", 3), ("sl", 4), ("end", 0), ("fin", 0),
+    ("d1", 0), ("select", 0), ("z0", 0), ("gr", 0), ("gl", 0), ("zf", 1), ("zf", -1),
+    ("select", 1), ("select", 7), ("ga", 0), ("hidden", 0), ("gr", 1), ("gl", 1), ("select", 6),
+    ("zf", 2), ("zf", -2), ("select", 2), ("ga", 1), ("rb", 0), ("ra", 0), ("gr", 7), ("gl", 7),
+    ("hidden", 1), ("ga", 7), ("zf", 3), ("select", 3), ("select", 5), ("gr", 6), ("gl", 6),
+    ("rl", 0), ("hidden", 7), ("ra", 1), ("rb", 1), ("ga", 6), ("gl", 2), ("gr", 2),
+    ("select", 4), ("sb", 0), ("sa", 0), ("hidden", 6), ("ra", 7), ("rb", 7), ("ga", 2),
+    ("gl", 3), ("gr", 3), ("rl", 1), ("hidden", 2), ("ra", 6), ("rb", 6), ("back", 0), ("gr", 5),
+    ("gl", 5), ("rl", 7), ("ga", 3), ("sb", 1), ("sa", 1), ("ga", 5), ("ra", 2), ("rb", 2),
+    ("gl", 4), ("gr", 4), ("sp", 0), ("rl", 6), ("hidden", 3), ("ga", 4), ("hidden", 5),
+    ("sb", 7), ("sa", 7), ("back", 1), ("sb", 6), ("rl", 2), ("sa", 6), ("ra", 3), ("rb", 3),
+    ("hidden", 4), ("sl", 0), ("ra", 5), ("rb", 5), ("sp", 1), ("back", 7), ("sb", 2), ("sa", 2),
+    ("back", 6), ("rl", 3), ("sp", 7), ("rl", 5), ("ra", 4), ("sl", 1), ("rb", 4), ("back", 2),
+    ("sp", 6), ("sb", 3), ("sa", 3), ("sa", 5), ("sb", 5), ("rl", 4), ("sp", 2), ("sl", 7),
+    ("back", 3), ("back", 5), ("sb", 4), ("sa", 4), ("sl", 6), ("sp", 3), ("sl", 2), ("sp", 5),
+    ("back", 4), ("sl", 3), ("sp", 4), ("sl", 5), ("sl", 4), ("end", 0), ("fin", 0),
 )
 F32, BF16 = jnp.float32, jnp.bfloat16
 
@@ -41,7 +42,7 @@
 
 def kernel(
     grad, ids, comb, dw_hbm, gw_hbm, uw_hbm, gs_hbm, us_hbm, out,
-    dw, gw, uw, gs, us, tok, t2, rows, lhs, hp32, hp, xo, xl, xr, hf, gg, ug, sg, yb, pb, yr, zs, zr, fin, fr,
+    dw, gw, uw, gs, us, tok, t2, rows, lhs, hp32, hp, xo, xl, xr, hf, gg, ug, sg, yb, pb, yr, zs, zr, zs_far, zr_far, fin, fr,
     load_sem, send_sem, recv_sem,
 ):
     d, e, t = lax.axis_index("dp"), lax.axis_index("expert"), lax.axis_index("etp")
@@ -310,6 +311,9 @@
         r = CHUNKS[k]
         if r == 0:
             zr[0] = total
+        elif abs(r) >= FAR:
+            zs_far[k] = total.astype(BF16)
+            returns.append(send(zs_far.at[k], zr_far.at[(-r) % NZ - FAR], at_z(r)))
         else:
             zs[k] = total
             returns.append(send(zs.at[k], zr.at[(-r) % NZ], at_z(r)))
@@ -327,7 +331,14 @@
             copy.wait_recv()
 
         def combine(h):
-            value = zr[:, :, h * fh : (h + 1) * fh].reshape(NZ * ROWS, fh)
+            cols = slice(h * fh, (h + 1) * fh)
+            value = jnp.concatenate(
+                [
+                    zr_far[j - FAR, :, cols].astype(F32) if FAR <= j <= NZ - FAR else zr[j, :, cols]
+                    for j in range(NZ)
+                ],
+                axis=0,
+            )
             coarse = value.astype(BF16)
             fine = (value - coarse.astype(F32)).astype(BF16)
             dims = (((0,), (0,)), ((), ()))
@@ -405,6 +416,8 @@
             vmem((n, NY - 1, ROWS, fq), BF16),
             vmem((n, ROWS, fq), F32),
             vmem((NZ, ROWS, fq), F32),
+            vmem((n, ROWS, fq), BF16),
+            vmem((NZ - 2 * FAR + 1, ROWS, fq), BF16),
             vmem((64, fh), BF16),
             vmem((64, fh), BF16),
             pltpu.SemaphoreType.DMA((5,)),

time: 108 us -> 97.8 us (0.906)
  Pallas kernels: 106 us -> 96.1 us
    pallas_call x1, Pallas kernels: 106 us -> 96.1 us  [on_device(): pl.pallas_call(kernel, out_shape=jax.ShapeDtypeStruct((tokens, width), BF...]
where the time goes in v4:
time: 97.8 us; the launch traced here: 97.6 us
  Pallas kernels  96.1 us (98%)
  local copies, waits for them, and re-layouts  1.54 us (2%)
    pallas_call x1, Pallas kernels, on_device(): pl.pallas_call(kernel, out_shape=jax.ShapeDtypeStruct((tokens, width), BF...  96.1 us

profile of v4, /device:TPU:1, one launch (start us, length us, event | category | flops | bytes accessed | tf_op | source)
XLA Modules:
  0.0 97.6 jit_solution(14113304471894249737)
XLA Ops:
  0.0 96.1 %shard_map.82 = bf16[8,6144]{1,0:T(8,128)(2,1)} custom-call(bf16[8,6144]{1,0:T(8,128)(2,1)} %grad.1, s32[4,8]{1,0:T(4,128)} %bitcast.12, bf16[4,8]{1,0:T(4,128)(2,1)} %bitcast.13, bf16[768,1536]{1,0:T(8,128)(2,1)} %bitcast.7, bf16[1536,768]{1,0:T(8,128)(2,1)} %bitcast.8, bf16[1536,768]{1,0:T(8,128)(2,1)} %bitcast.9, bf16[1536,768]{1,0:T(8,128)(2,1)} %bitcast.10, ...), custom_call_target="tpu_custom_call" | custom-call | flops 10871635968 | bytes 12000000 | tf_op jit(solution)/shard_map/pallas_call | solution.py:390
  96.1 1.5 %copy.10 = bf16[8,6144]{1,0:T(8,128)(2,1)} copy(bf16[8,6144]{1,0:T(8,128)(2,1)} %shard_map.82) | data formatting | bytes 196608

commit v5 on v4

--- a/solution.py
+++ b/solution.py
@@ -11,23 +11,23 @@
 ROWS = NX * CAP
 META = 128
 FAR = 3
-CHUNKS = (0, 1, -2, 3, 4, -3, 2, -1)
+CHUNKS = (0, 1, -1, 4, 3, -3, 2, -2)
 ORDER = (
-    ("d1", 0), ("select", 0), ("z0", 0), ("gr", 0), ("gl", 0), ("zf", 1), ("zf", -1),
-    ("select", 1), ("select", 7), ("ga", 0), ("hidden", 0), ("gr", 1), ("gl", 1), ("select", 6),
-    ("zf", 2), ("zf", -2), ("select", 2), ("ga", 1), ("rb", 0), ("ra", 0), ("gr", 7), ("gl", 7),
-    ("hidden", 1), ("ga", 7), ("zf", 3), ("select", 3), ("select", 5), ("gr", 6), ("gl", 6),
-    ("rl", 0), ("hidden", 7), ("ra", 1), ("rb", 1), ("ga", 6), ("gl", 2), ("gr", 2),
-    ("select", 4), ("sb", 0), ("sa", 0), ("hidden", 6), ("ra", 7), ("rb", 7), ("ga", 2),
-    ("gl", 3), ("gr", 3), ("rl", 1), ("hidden", 2), ("ra", 6), ("rb", 6), ("back", 0), ("gr", 5),
-    ("gl", 5), ("rl", 7), ("ga", 3), ("sb", 1), ("sa", 1), ("ga", 5), ("ra", 2), ("rb", 2),
-    ("gl", 4), ("gr", 4), ("sp", 0), ("rl", 6), ("hidden", 3), ("ga", 4), ("hidden", 5),
-    ("sb", 7), ("sa", 7), ("back", 1), ("sb", 6), ("rl", 2), ("sa", 6), ("ra", 3), ("rb", 3),
-    ("hidden", 4), ("sl", 0), ("ra", 5), ("rb", 5), ("sp", 1), ("back", 7), ("sb", 2), ("sa", 2),
-    ("back", 6), ("rl", 3), ("sp", 7), ("rl", 5), ("ra", 4), ("sl", 1), ("rb", 4), ("back", 2),
-    ("sp", 6), ("sb", 3), ("sa", 3), ("sa", 5), ("sb", 5), ("rl", 4), ("sp", 2), ("sl", 7),
-    ("back", 3), ("back", 5), ("sb", 4), ("sa", 4), ("sl", 6), ("sp", 3), ("sl", 2), ("sp", 5),
-    ("back", 4), ("sl", 3), ("sp", 4), ("sl", 5), ("sl", 4), ("end", 0), ("fin", 0),
+    ("d1", 0), ("select", 0), ("z0", 0), ("ga", 0), ("select", 2), ("zf", 1), ("zf", -1),
+    ("gl", 0), ("gr", 0), ("select", 1), ("hidden", 0), ("ga", 2), ("select", 6), ("zf", 2),
+    ("zf", -2), ("select", 7), ("gl", 2), ("gr", 2), ("ra", 0), ("rb", 0), ("ga", 1),
+    ("hidden", 2), ("gl", 1), ("gr", 1), ("rl", 0), ("zf", 3), ("select", 5), ("select", 4),
+    ("ga", 6), ("hidden", 1), ("ra", 2), ("rb", 2), ("gl", 6), ("gr", 6), ("ga", 7), ("sb", 0),
+    ("sa", 0), ("hidden", 6), ("ra", 1), ("rb", 1), ("gl", 7), ("gr", 7), ("select", 3),
+    ("rl", 2), ("ga", 5), ("hidden", 7), ("ra", 6), ("rb", 6), ("gl", 5), ("gr", 5), ("back", 0),
+    ("ga", 4), ("rl", 1), ("sa", 2), ("gl", 4), ("gr", 4), ("sb", 2), ("hidden", 5), ("ra", 7),
+    ("rb", 7), ("sp", 0), ("ga", 3), ("hidden", 4), ("gl", 3), ("gr", 3), ("rl", 6), ("sb", 1),
+    ("sa", 1), ("back", 2), ("ra", 5), ("sl", 0), ("rb", 5), ("rl", 7), ("ra", 4), ("rb", 4),
+    ("hidden", 3), ("sp", 2), ("sb", 6), ("sa", 6), ("back", 1), ("sa", 7), ("sb", 7), ("rl", 5),
+    ("rl", 4), ("sl", 2), ("rb", 3), ("ra", 3), ("sp", 1), ("back", 6), ("sa", 5), ("sb", 5),
+    ("back", 7), ("sp", 6), ("sl", 1), ("sa", 4), ("sb", 4), ("rl", 3), ("back", 5), ("sp", 7),
+    ("back", 4), ("sp", 5), ("sl", 6), ("sa", 3), ("sb", 3), ("sp", 4), ("sl", 7), ("back", 3),
+    ("sl", 5), ("sp", 3), ("sl", 4), ("sl", 3), ("end", 0), ("fin", 0),
 )
 F32, BF16 = jnp.float32, jnp.bfloat16
 
@@ -42,7 +42,7 @@
 
 def kernel(
     grad, ids, comb, dw_hbm, gw_hbm, uw_hbm, gs_hbm, us_hbm, out,
-    dw, gw, uw, gs, us, tok, t2, rows, lhs, hp32, hp, xo, xl, xr, hf, gg, ug, sg, yb, pb, yr, zs, zr, zs_far, zr_far, fin, fr,
+    dw, gw, uw, gs, us, tok, t2, rows, lhs, hp32, hp, xo, xl, xr, hf, gg, ug, sg, yb, pb, yr, zs, zr, zs_far, zr_far, mixes, fin, fr,
     load_sem, send_sem, recv_sem,
 ):
     d, e, t = lax.axis_index("dp"), lax.axis_index("expert"), lax.axis_index("etp")
@@ -138,6 +138,7 @@
             arrived(copy)
         gather[1] = send(t2.at[0], t2.at[1], at_z(-1))
         gather[-1] = send(t2.at[0], t2.at[NZ - 1], at_z(1))
+        prepare()
 
     def zf(r):
         arrived(gather[r])
@@ -186,7 +187,8 @@
             )
             rows[k, t, :, h * fh : (h + 1) * fh] = part.astype(BF16)
         block = rows.at[k, t]
-        state[k]["ag"] = [send(block, block, device) for device in (at_y(1), at_y(-1), at_y(2))]
+        far = send(block, block, at_y(2))
+        state[k]["ag"] = [send(block, block, at_y(1)), send(block, block, at_y(-1)), far]
         state[k]["sib"] = [send(block, block, sibling)]
 
     def pass_on(k, i, there):
@@ -284,20 +286,21 @@
             ug[:, cols] = (h * gate * s).astype(BF16)
 
         tile = 512 if fq % 512 == 0 else min(256, fq)
-
-        @pl.loop(0, fq // tile)
-        def _(n):
-            cols = pl.ds(pl.multiple_of(n * tile, tile), tile)
+        state[k]["pair"] = []
+        for start in range(0, fq, tile):
+            cols = slice(start, start + tile)
             part = dot_nt(gg[...], gw[cols, :]) + dot_nt(ug[...], uw[cols, :])
             for i in range(NT):
                 sg[k, i // 2, i % 2, :, cols] = part[i * ROWS : (i + 1) * ROWS]
-
-        state[k]["pair"] = send(sg.at[k, :, 1 - c], yb.at[k], sibling)
+            state[k]["pair"].append(
+                send(sg.at[k, :, 1 - c, :, cols], yb.at[k, :, :, cols], sibling)
+            )
 
     def sp(k):
-        state[k]["pair"].wait_recv()
+        for copy in state[k]["pair"]:
+            copy.wait_recv()
         state[k]["ys"] = []
-        for i in range(1, NY):
+        for i in (2, 1, 3):
             q = lax.rem(y + i, NY)
             pb[k, i - 1] = (sg[k, q, c] + yb[k, q]).astype(BF16)
             state[k]["ys"].append(send(pb.at[k, i - 1], yr.at[k, i - 1], at_y(i)))
@@ -318,7 +321,7 @@
             zs[k] = total
             returns.append(send(zs.at[k], zr.at[(-r) % NZ], at_z(r)))
 
-    def end(_):
+    def prepare():
         meta = meta_of(0)
         mix = [[], []]
         for j in range(NZ):
@@ -326,7 +329,10 @@
             code, weight = meta_row(meta, x), meta_row(meta, x + NZ)
             for h in range(2):
                 mix[h].append(jnp.where(choose(code, h), weight, 0.0))
-        mix = [jnp.concatenate(m, axis=0).astype(BF16) for m in mix]
+        for h in range(2):
+            mixes[h] = jnp.concatenate(mix[h], axis=0).astype(BF16)
+
+    def end(_):
         for copy in returns:
             copy.wait_recv()
 
@@ -342,8 +348,8 @@
             coarse = value.astype(BF16)
             fine = (value - coarse.astype(F32)).astype(BF16)
             dims = (((0,), (0,)), ((), ()))
-            return lax.dot_general(mix[h], coarse, dims, preferred_element_type=F32) + lax.dot_general(
-                mix[h], fine, dims, preferred_element_type=F32
+            return lax.dot_general(mixes[h], coarse, dims, preferred_element_type=F32) + lax.dot_general(
+                mixes[h], fine, dims, preferred_element_type=F32
             )
 
         fin[...] = (combine(0) + combine(1)).astype(BF16)
@@ -372,7 +378,7 @@
         copy.wait_send()
 
 
-COPIES = 3 + 7 + 8 * (4 + 3 + 4 + 2 + 2 + 2 + 1 + 3) + 7 + 3
+COPIES = 3 + 7 + 8 * (4 + 3 + 4 + 2 + 2 + 2 + 3 + 3) + 7 + 3
 
 
 def on_device(
@@ -418,6 +424,7 @@
             vmem((NZ, ROWS, fq), F32),
             vmem((n, ROWS, fq), BF16),
             vmem((NZ - 2 * FAR + 1, ROWS, fq), BF16),
+            vmem((2, NZ * ROWS, 64), BF16),
             vmem((64, fh), BF16),
             vmem((64, fh), BF16),
             pltpu.SemaphoreType.DMA((5,)),

time: 97.8 us -> 99.6 us (1.018)
  Pallas kernels: 96.1 us -> 98 us
    pallas_call x1, Pallas kernels: 96.1 us -> 98 us  [on_device(): pl.pallas_call(kernel, out_shape=jax.ShapeDtypeStruct((tokens, width), BF...]
where the time goes in v5:
time: 99.6 us; the launch traced here: 99.5 us
  Pallas kernels  98 us (98%)
  local copies, waits for them, and re-layouts  1.54 us (2%)
    pallas_call x1, Pallas kernels, on_device(): pl.pallas_call(kernel, out_shape=jax.ShapeDtypeStruct((tokens, width), BF...  98 us

profile of v5, /device:TPU:1, one launch (start us, length us, event | category | flops | bytes accessed | tf_op | source)
XLA Modules:
  0.0 99.5 jit_solution(15972070922110121084)
XLA Ops:
  0.0 98.0 %shard_map.82 = bf16[8,6144]{1,0:T(8,128)(2,1)} custom-call(bf16[8,6144]{1,0:T(8,128)(2,1)} %grad.1, s32[4,8]{1,0:T(4,128)} %bitcast.12, bf16[4,8]{1,0:T(4,128)(2,1)} %bitcast.13, bf16[768,1536]{1,0:T(8,128)(2,1)} %bitcast.7, bf16[1536,768]{1,0:T(8,128)(2,1)} %bitcast.8, bf16[1536,768]{1,0:T(8,128)(2,1)} %bitcast.9, bf16[1536,768]{1,0:T(8,128)(2,1)} %bitcast.10, ...), custom_call_target="tpu_custom_call" | custom-call | flops 10871635968 | bytes 12000000 | tf_op jit(solution)/shard_map/pallas_call | solution.py:396
  98.0 1.5 %copy.10 = bf16[8,6144]{1,0:T(8,128)(2,1)} copy(bf16[8,6144]{1,0:T(8,128)(2,1)} %shard_map.82) | data formatting | bytes 196608

commit v6 on v4

--- a/solution.py
+++ b/solution.py
@@ -42,7 +42,7 @@
 
 def kernel(
     grad, ids, comb, dw_hbm, gw_hbm, uw_hbm, gs_hbm, us_hbm, out,
-    dw, gw, uw, gs, us, tok, t2, rows, lhs, hp32, hp, xo, xl, xr, hf, gg, ug, sg, yb, pb, yr, zs, zr, zs_far, zr_far, fin, fr,
+    dw, gw, uw, gs, us, tok, t2, rows, lhs, hp32, hp, xo, xl, xr, hf, gg, ug, sg, yb, pb, yr, zs, zr, zs_far, zr_far, mixes, fin, fr,
     load_sem, send_sem, recv_sem,
 ):
     d, e, t = lax.axis_index("dp"), lax.axis_index("expert"), lax.axis_index("etp")
@@ -138,6 +138,7 @@
             arrived(copy)
         gather[1] = send(t2.at[0], t2.at[1], at_z(-1))
         gather[-1] = send(t2.at[0], t2.at[NZ - 1], at_z(1))
+        prepare()
 
     def zf(r):
         arrived(gather[r])
@@ -186,7 +187,8 @@
             )
             rows[k, t, :, h * fh : (h + 1) * fh] = part.astype(BF16)
         block = rows.at[k, t]
-        state[k]["ag"] = [send(block, block, device) for device in (at_y(1), at_y(-1), at_y(2))]
+        far = send(block, block, at_y(2))
+        state[k]["ag"] = [send(block, block, at_y(1)), send(block, block, at_y(-1)), far]
         state[k]["sib"] = [send(block, block, sibling)]
 
     def pass_on(k, i, there):
@@ -297,7 +299,7 @@
     def sp(k):
         state[k]["pair"].wait_recv()
         state[k]["ys"] = []
-        for i in range(1, NY):
+        for i in (2, 1, 3):
             q = lax.rem(y + i, NY)
             pb[k, i - 1] = (sg[k, q, c] + yb[k, q]).astype(BF16)
             state[k]["ys"].append(send(pb.at[k, i - 1], yr.at[k, i - 1], at_y(i)))
@@ -318,7 +320,7 @@
             zs[k] = total
             returns.append(send(zs.at[k], zr.at[(-r) % NZ], at_z(r)))
 
-    def end(_):
+    def prepare():
         meta = meta_of(0)
         mix = [[], []]
         for j in range(NZ):
@@ -326,7 +328,10 @@
             code, weight = meta_row(meta, x), meta_row(meta, x + NZ)
             for h in range(2):
                 mix[h].append(jnp.where(choose(code, h), weight, 0.0))
-        mix = [jnp.concatenate(m, axis=0).astype(BF16) for m in mix]
+        for h in range(2):
+            mixes[h] = jnp.concatenate(mix[h], axis=0).astype(BF16)
+
+    def end(_):
         for copy in returns:
             copy.wait_recv()
 
@@ -342,8 +347,8 @@
             coarse = value.astype(BF16)
             fine = (value - coarse.astype(F32)).astype(BF16)
             dims = (((0,), (0,)), ((), ()))
-            return lax.dot_general(mix[h], coarse, dims, preferred_element_type=F32) + lax.dot_general(
-                mix[h], fine, dims, preferred_element_type=F32
+            return lax.dot_general(mixes[h], coarse, dims, preferred_element_type=F32) + lax.dot_general(
+                mixes[h], fine, dims, preferred_element_type=F32
             )
 
         fin[...] = (combine(0) + combine(1)).astype(BF16)
@@ -418,6 +423,7 @@
             vmem((NZ, ROWS, fq), F32),
             vmem((n, ROWS, fq), BF16),
             vmem((NZ - 2 * FAR + 1, ROWS, fq), BF16),
+            vmem((2, NZ * ROWS, 64), BF16),
             vmem((64, fh), BF16),
             vmem((64, fh), BF16),
             pltpu.SemaphoreType.DMA((5,)),

time: 97.8 us -> 99.2 us (1.014)
  no operation moved by 1% of the time
where the time goes in v6:
time: 99.2 us; the launch traced here: 98.6 us
  Pallas kernels  97 us (98%)
  local copies, waits for them, and re-layouts  1.54 us (2%)
    pallas_call x1, Pallas kernels, on_device(): pl.pallas_call(kernel, out_shape=jax.ShapeDtypeStruct((tokens, width), BF...  97 us

profile of v6, /device:TPU:1, one launch (start us, length us, event | category | flops | bytes accessed | tf_op | source)
XLA Modules:
  0.0 98.6 jit_solution(6886143014551892867)
XLA Ops:
  0.0 97.0 %shard_map.82 = bf16[8,6144]{1,0:T(8,128)(2,1)} custom-call(bf16[8,6144]{1,0:T(8,128)(2,1)} %grad.1, s32[4,8]{1,0:T(4,128)} %bitcast.12, bf16[4,8]{1,0:T(4,128)(2,1)} %bitcast.13, bf16[768,1536]{1,0:T(8,128)(2,1)} %bitcast.7, bf16[1536,768]{1,0:T(8,128)(2,1)} %bitcast.8, bf16[1536,768]{1,0:T(8,128)(2,1)} %bitcast.9, bf16[1536,768]{1,0:T(8,128)(2,1)} %bitcast.10, ...), custom_call_target="tpu_custom_call" | custom-call | flops 10871635968 | bytes 12000000 | tf_op jit(solution)/shard_map/pallas_call | solution.py:395
  97.0 1.5 %copy.10 = bf16[8,6144]{1,0:T(8,128)(2,1)} copy(bf16[8,6144]{1,0:T(8,128)(2,1)} %shard_map.82) | data formatting | bytes 196608

commit v7 on v6

--- a/solution.py
+++ b/solution.py
@@ -138,12 +138,13 @@
             arrived(copy)
         gather[1] = send(t2.at[0], t2.at[1], at_z(-1))
         gather[-1] = send(t2.at[0], t2.at[NZ - 1], at_z(1))
-        prepare()
 
     def zf(r):
         arrived(gather[r])
         if r > 0:
             gather[r + 1] = send(t2.at[r], t2.at[r + 1], at_z(-1))
+            if r == 2:
+                prepare()
         else:
             gather[r - 1] = send(t2.at[NZ + r], t2.at[NZ + r - 1], at_z(1))
 
@@ -187,8 +188,7 @@
             )
             rows[k, t, :, h * fh : (h + 1) * fh] = part.astype(BF16)
         block = rows.at[k, t]
-        far = send(block, block, at_y(2))
-        state[k]["ag"] = [send(block, block, at_y(1)), send(block, block, at_y(-1)), far]
+        state[k]["ag"] = [send(block, block, device) for device in (at_y(1), at_y(-1), at_y(2))]
         state[k]["sib"] = [send(block, block, sibling)]
 
     def pass_on(k, i, there):
@@ -299,7 +299,7 @@
     def sp(k):
         state[k]["pair"].wait_recv()
         state[k]["ys"] = []
-        for i in (2, 1, 3):
+        for i in range(1, NY):
             q = lax.rem(y + i, NY)
             pb[k, i - 1] = (sg[k, q, c] + yb[k, q]).astype(BF16)
             state[k]["ys"].append(send(pb.at[k, i - 1], yr.at[k, i - 1], at_y(i)))

time: 99.2 us -> 97.7 us (0.985)
  Pallas kernels: 97 us -> 96 us
    pallas_call x1, Pallas kernels: 97 us -> 96 us  [on_device(): pl.pallas_call(kernel, out_shape=jax.ShapeDtypeStruct((tokens, width), BF...]
where the time goes in v7:
time: 97.7 us; the launch traced here: 97.5 us
  Pallas kernels  96 us (98%)
  local copies, waits for them, and re-layouts  1.54 us (2%)
    pallas_call x1, Pallas kernels, on_device(): pl.pallas_call(kernel, out_shape=jax.ShapeDtypeStruct((tokens, width), BF...  96 us

profile of v7, /device:TPU:1, one launch (start us, length us, event | category | flops | bytes accessed | tf_op | source)
XLA Modules:
  0.0 97.5 jit_solution(3738966767342663339)
XLA Ops:
  0.0 96.0 %shard_map.82 = bf16[8,6144]{1,0:T(8,128)(2,1)} custom-call(bf16[8,6144]{1,0:T(8,128)(2,1)} %grad.1, s32[4,8]{1,0:T(4,128)} %bitcast.12, bf16[4,8]{1,0:T(4,128)(2,1)} %bitcast.13, bf16[768,1536]{1,0:T(8,128)(2,1)} %bitcast.7, bf16[1536,768]{1,0:T(8,128)(2,1)} %bitcast.8, bf16[1536,768]{1,0:T(8,128)(2,1)} %bitcast.9, bf16[1536,768]{1,0:T(8,128)(2,1)} %bitcast.10, ...), custom_call_target="tpu_custom_call" | custom-call | flops 10871635968 | bytes 12000000 | tf_op jit(solution)/shard_map/pallas_call | solution.py:395
  96.0 1.5 %copy.10 = bf16[8,6144]{1,0:T(8,128)(2,1)} copy(bf16[8,6144]{1,0:T(8,128)(2,1)} %shard_map.82) | data formatting | bytes 196608
